TPU v7x, 32 devices: a whole 2x2x4 slice. The times are simulated.
32 devices in a mesh: seq: 8 (over z, x), tp: 4 (over y, core).
Axes of the slice: x: 2, y: 2, z: 4, core: 2. Of those that a mesh axis runs over, the one named last changes fastest.
Arguments:
- mr_qkv: bfloat16 [8192, 3, 4096], P('seq', None, 'tp'), may hold values from -6 to 6
- residual_in: bfloat16 [8192, 4096], P('seq', 'tp'), may hold values from -6 to 6
- mr_short: float32 [7, 3, 4096], P(None, None, 'tp'), may hold values from -2 to 2
- mr_filter: bfloat16 [128, 4096], P(None, 'tp'), may hold values from -0.5 to 0.5
- mr_out: bfloat16 [4096, 4096], P('seq', 'tp'), may hold values from -0.09375 to 0.09375
- norm_gain: float32 [4096], replicated, may hold values from 0.5 to 1.5
- lr_in: bfloat16 [4096, 3, 4096], P('seq', None, 'tp'), may hold values from -0.09375 to 0.09375
- lr_short: float32 [7, 3, 4096], P(None, None, 'tp'), may hold values from -2 to 2
- lr_rate: float32 [16, 4096], P(None, 'tp'), may hold values from 0 to 1, as said below
- lr_residue: float32 [16, 4096], P(None, 'tp'), may hold values from -1.5 to 1.5
Outputs:
- stream: bfloat16 [8192, 4096], P('seq', 'tp')
- lr_gated: bfloat16 [8192, 4096], P('seq', 'tp')
Inputs may be any that keep to these rules, and one draw needn't show every extreme that they name: `lr_rate`: every rate is positive.
All inputs are finite; a program needn't handle non-finite values.
Results may differ from a plain program's by a relative error of at most 0.014.
Values may be sent and summed in bfloat16 or wider, within the bound.
No kernel may reach another device: no remote copies, remote signals or barrier semaphores. Data moves between devices by JAX's collectives and lax.ppermute only.
A program may use at most 192 MiB of HBM per device.

v0:
```python
import jax
import jax.numpy as jnp
from jax import lax
from jax.sharding import PartitionSpec as P

norm_eps = 1e-06
block_rows = 64


def entering_2(x, axis, join, neutral):
    place = lax.axis_index(axis)
    gathered = jax.tree.map(
        lambda a, kind: lax.all_gather(a.astype(kind), axis), x, (jnp.bfloat16, jnp.bfloat16)
    )
    state = jax.tree.map(lambda a, e: jnp.zeros_like(a) + jnp.asarray(e, a.dtype), x, neutral)

    def one(step, state):
        return join(
            state,
            jax.tree.map(
                lambda a, own: lax.dynamic_index_in_dim(a, step, 0, False).astype(own.dtype),
                gathered,
                x,
            ),
        )

    return lax.fori_loop(0, place, one, state)


def from_behind(value, axis, steps):
    count = lax.axis_size(axis)
    initial, last = (max(0, -steps), min(count, count - steps))
    return lax.ppermute(value, axis, [(source, source + steps) for source in range(initial, last)])


def featurize(extended, taps, row_count):
    total = jnp.zeros((row_count,) + extended.shape[1:], jnp.float32)
    width = taps.shape[0]
    for tap_index in range(width):
        begin = width - 1 - tap_index
        total = total + taps[tap_index] * extended[begin : begin + row_count].astype(jnp.float32)
    return total


def depthwise(extended, filters):
    flipped = filters[::-1][:, None, :]
    result = lax.conv_general_dilated(
        extended[None],
        flipped,
        (1,),
        [(0, 0)],
        dimension_numbers=("NWC", "WIO", "NWC"),
        feature_group_count=filters.shape[1],
        preferred_element_type=jnp.float32,
    )
    return result[0]


def lr_tables(rate, residue):
    coef = residue * jnp.sqrt(2.0 * rate)
    lags = jnp.arange(block_rows).astype(jnp.float32)
    filter_lags = jnp.sum(coef[None] * jnp.exp(-rate[None] * lags[:, None, None]), axis=1)
    places = jnp.arange(block_rows, dtype=jnp.int32)
    spread = places[:, None] - places[None, :]
    toeplitz = jnp.where(
        (spread >= 0)[:, :, None], jnp.take(filter_lags, jnp.maximum(spread, 0), axis=0), 0.0
    )
    into_state = jnp.exp(-rate[None] * (block_rows - 1.0 - lags)[:, None, None])
    from_state = coef[None] * jnp.exp(-rate[None] * (lags + 1.0)[:, None, None])
    step_decay = jnp.exp(-rate * block_rows)
    return (toeplitz, into_state, from_state, step_decay)


def chain_combine(earlier, later):
    return (earlier[0] * later[0], later[0] * earlier[1] + later[1])


def long_conv(values, rate, residue):
    toeplitz, into_state, from_state, step_decay = lr_tables(rate, residue)
    rows = values.shape[0]
    group = values.shape[1]
    high = lax.Precision.HIGHEST
    count = rows // block_rows
    blocks = values.reshape(count, block_rows, group)
    inside = jnp.einsum("ijc,bjc->bic", toeplitz, blocks, precision=high)
    block_sums = jnp.einsum("jnc,bjc->bnc", into_state, blocks, precision=high)

    def advance(carried, block_sum):
        return (step_decay * carried + block_sum, carried)

    start_state = jnp.zeros((rate.shape[0], group), jnp.float32)
    end_state, entering = lax.scan(advance, start_state, block_sums)
    device_decay = jnp.exp(-rate * rows)
    prefix = entering_2(
        (device_decay, end_state), "seq", chain_combine, (jnp.ones_like(rate), jnp.zeros_like(rate))
    )
    incoming = prefix[1]
    offsets = jnp.arange(count).astype(jnp.float32)
    entering = (
        entering + jnp.exp(-rate[None] * block_rows * offsets[:, None, None]) * incoming[None]
    )
    outside = jnp.einsum("inc,bnc->bic", from_state, entering, precision=high)
    return (inside + outside).reshape(rows, group)


def per_device(
    mr_qkv,
    residual_in,
    mr_short,
    mr_filter,
    mr_out,
    norm_gain,
    lr_in,
    lr_short,
    lr_rate,
    lr_residue,
):
    rows = mr_qkv.shape[0]
    channels = mr_qkv.shape[2]
    short_len = mr_short.shape[0]
    medium_len = mr_filter.shape[0]
    short_rim = from_behind(mr_qkv[rows - (short_len - 1) :], "seq", 1)
    featured = featurize(jnp.concatenate([short_rim, mr_qkv], axis=0), mr_short, rows)
    queries = featured[:, 0]
    product = (featured[:, 1] * featured[:, 2]).astype(jnp.bfloat16)
    prior = from_behind(product[rows - (medium_len - 1) :], "seq", 1)
    extended_u = jnp.concatenate([prior, product], axis=0)
    medium = depthwise(extended_u, mr_filter)
    mr_gated = (queries * medium).astype(jnp.bfloat16)
    mixed = lax.all_gather(mr_gated, "tp", axis=1, tiled=True)
    pieces = lax.all_gather(mr_out, "seq", axis=0, tiled=True)
    columns = lax.slice_in_dim(mixed, 0, pieces.shape[0], axis=1)
    projected = jnp.zeros((rows, channels), jnp.float32) + jnp.dot(
        columns, pieces, preferred_element_type=jnp.float32
    )
    stream = (residual_in.astype(jnp.float32) + projected).astype(jnp.bfloat16)
    values = stream.astype(jnp.float32)
    squares = lax.psum(jnp.sum(values * values, axis=1), "tp")
    full_width = channels * lax.axis_size("tp")
    scale = lax.rsqrt(squares / full_width + norm_eps)
    own_gain = lax.dynamic_slice_in_dim(norm_gain, lax.axis_index("tp") * channels, channels)
    normed = (values * scale[:, None] * own_gain).astype(jnp.bfloat16)
    features = lax.all_gather(normed, "tp", axis=1, tiled=True)
    pieces = lax.all_gather(lr_in, "seq", axis=0, tiled=True)
    columns = lax.slice_in_dim(features, 0, pieces.shape[0], axis=1)
    lr_proj = jnp.zeros((rows, 3, channels), jnp.float32) + jnp.einsum(
        "tm,mgc->tgc", columns, pieces, preferred_element_type=jnp.float32
    )
    lr_qkv = lr_proj.astype(jnp.bfloat16)
    lr_rim = from_behind(lr_qkv[rows - (short_len - 1) :], "seq", 1)
    lr_feat = featurize(jnp.concatenate([lr_rim, lr_qkv], axis=0), lr_short, rows)
    lr_u = (lr_feat[:, 1] * lr_feat[:, 2]).astype(jnp.bfloat16)
    conv = long_conv(lr_u.astype(jnp.float32), lr_rate, lr_residue)
    lr_gated = (lr_feat[:, 0] * conv).astype(jnp.bfloat16)
    return (stream, lr_gated)


def solution(mesh):
    placed = (
        P("seq", None, "tp"),
        P("seq", "tp"),
        P(None, None, "tp"),
        P(None, "tp"),
        P("seq", "tp"),
        P(),
        P("seq", None, "tp"),
        P(None, None, "tp"),
        P(None, "tp"),
        P(None, "tp"),
    )
    return jax.shard_map(
        per_device,
        mesh=mesh,
        in_specs=placed,
        out_specs=(P("seq", "tp"), P("seq", "tp")),
        check_vma=False,
    )
```

profile of v0, /device:TPU:0, one launch (start us, length us, event | category | flops | bytes accessed | tf_op | source)
XLA Modules:
  0.0 1231.6 jit_solution(5585978475956463347)
XLA Ops:
  17.5 19.4 %multiply_add_fusion.1 = f32[1024,3,1024]{2,0,1:T(8,128)S(1)} fusion(bf16[1024,3,1024]{2,0,1:T(8,128)(2,1)} %param.14, bf16[6,3,1024]{2,0,1:T(8,128)(2,1)S(1)} %collective-permute-done, f32[3,1024]{1,0:T(4,128)S(1)} %get-tuple-element.157, f32[3,1024]{1,0:T(4,128)S(1)} %get-tuple-element.158, f32[3,1024]{1,0:T(4,128)S(1)} %get-tuple-element.159, ...), kind=kLoop, calls=%fused_computation.23 | loop fusion | flops 119537664 | bytes 18997248 | tf_op jit(solution)/shard_map/add | solution.py:41
  50.0 159.2 %broadcast_select_fusion = f32[8,144,1024]{2,0,1:T(8,128)S(1)} fusion(pred[8,144]{0,1:T(8,128)(4,1)S(1)} %copy-done.8, bf16[128,1,1024]{2,0,1:T(8,128)(2,1)S(1)} %bitcast.111, bf16[8,271,1024]{2,0,1:T(8,128)(2,1)S(1)} %fusion.79), kind=kOutput, calls=%fused_computation.86 | convolution fusion | flops 303169536 | bytes 9421952 | tf_op jit(solution)/shard_map/conv_general_dilated | solution.py:47
  217.6 57.0 %all-gather.7.cloned.1.call-done = bf16[1024,4096]{1,0:T(8,128)(2,1)} async-done(((bf16[1024,1024]{1,0:T(8,128)(2,1)}), bf16[1024,4096]{1,0:T(8,128)(2,1)}) %all-gather.7.cloned.1.call-update) | async-done | bytes 8388624 | tf_op jit(solution)/shard_map/all_gather | solution.py:130
  274.6 127.1 %all-gather.9.cloned.1.call-done = bf16[4096,1024]{1,0:T(8,128)(2,1)} async-done(((bf16[512,1024]{1,0:T(8,128)(2,1)}), bf16[4096,1024]{1,0:T(8,128)(2,1)}) %all-gather.9.cloned.1.call-update) | async-done | bytes 8388624 | tf_op jit(solution)/shard_map/all_gather | solution.py:131
  401.7 14.3 %fusion.34 = (f32[1024]{0:T(1024)S(1)}, bf16[1024,1024]{0,1:T(8,128)(2,1)S(1)}) fusion(bf16[1024,4096]{1,0:T(8,128)(2,1)} %all-gather.7.cloned.1.call-done, bf16[4096,1024]{1,0:T(8,128)(2,1)} %all-gather.9.cloned.1.call-done, bf16[1024,1024]{0,1:T(8,128)(2,1)} %copy.39), kind=kOutput, calls=%fused_computation.63 | convolution fusion | flops 8596225024 | bytes 20975616 | tf_op jit(solution)/shard_map/dot_general | solution.py:133
  416.0 6.3 psum.7
  425.4 31.0 %all-gather = bf16[128,1024]{1,0:T(8,128)(2,1)S(1)} all-gather(bf16[16,1024]{1,0:T(8,128)(2,1)S(1)} %get-tuple-element.152), channel_id=2, replica_groups=mesh['seq'=8,'tp'=4] {'seq'}, dimensions={0}, use_global_device_ids=true | all-gather | bytes 294912 | tf_op jit(solution)/shard_map/all_gather | solution.py:13
  456.6 11.8 multiply_reduce_fusion
  468.4 12.2 all-gather.11.cloned.1.call-done
  480.6 481.9 %all-gather.13.cloned.1.call-done = bf16[4096,3,1024]{2,0,1:T(8,128)(2,1)} async-done(((bf16[512,3,1024]{2,0,1:T(8,128)(2,1)}), bf16[4096,3,1024]{2,0,1:T(8,128)(2,1)}) %all-gather.13.cloned.1.call-update) | async-done | bytes 25165840 | tf_op jit(solution)/shard_map/all_gather | solution.py:144
  962.4 33.0 %fusion.48 = bf16[1024,3,1024]{2,0,1:T(8,128)(2,1)S(1)} fusion(bf16[4096,3,1024]{2,0,1:T(8,128)(2,1)} %all-gather.13.cloned.1.call-done, bf16[1024,4096]{0,1:T(8,128)(2,1)} %all-gather.11.cloned.1.call-done), kind=kOutput, calls=%fused_computation.83 | convolution fusion | flops 25772949504 | bytes 39845888 | tf_op jit(solution)/shard_map/tm,mgc->tgc/dot_general | solution.py:146
  1001.0 18.5 %gather_fusion = f32[4096,1024]{1,0:T(8,128)} fusion(f32[64,1024]{1,0:T(8,128)S(1)} %copy.47, s32[4096]{0:T(1024)S(1)} %broadcast_clamp_fusion), kind=kCustom, calls=%fused_computation | custom fusion | bytes 33570816 | tf_op jit(solution)/shard_map/jit(_take)/gather | solution.py:66
  1019.5 30.5 %copy.48 = f32[64,64,1024]{1,0,2:T(8,128)} copy(f32[64,64,1024]{2,1,0:T(8,128)} %bitcast.105) | data formatting | bytes 33554432 | tf_op jit(solution)/shard_map/jit(_take)/gather | solution.py:66
  1053.9 19.3 %multiply_add_fusion = f32[1024,3,1024]{2,0,1:T(8,128)S(1)} fusion(bf16[1024,3,1024]{2,0,1:T(8,128)(2,1)} %copy-done.3, bf16[6,3,1024]{2,0,1:T(8,128)(2,1)S(1)} %collective-permute-done.2, f32[3,1024]{1,0:T(4,128)S(1)} %get-tuple-element.163, f32[3,1024]{1,0:T(4,128)S(1)} %get-tuple-element.164, f32[3,1024]{1,0:T(4,128)S(1)} %get-tuple-element.165, ...), kind=kLoop, calls=%fused_computation.22 | loop fusion | flops 119537664 | bytes 18997248 | tf_op jit(solution)/shard_map/add | solution.py:41
  1079.7 6.2 copy.49
  1085.8 11.0 fusion.51
  1096.8 6.0 copy.51
  1102.8 24.4 %while.26 = (s32[]{:T(128)}, f32[16,1024]{1,0:T(8,128)S(1)}, f32[16,16,1024]{2,1,0:T(8,128)}, f32[16,1024]{1,0:T(8,128)S(1)}, f32[16,16,1024]{2,1,0:T(8,128)}, /*index=5*/s32[]{:T(128)}, s32[]{:T(128)}) while((s32[]{:T(128)}, f32[16,1024]{1,0:T(8,128)S(1)}, f32[16,16,1024]{2,1,0:T(8,128)}, f32[16,1024]{1,0:T(8,128)S(1)}, ...), condition=%wide.region_4.5_spmd.clone, body=%wide.region_3.4_spmd.clone.sunk | while | flops 65539 | bytes 393820 | solution.py:92
  1127.2 31.0 %all-gather.1 = bf16[128,1024]{1,0:T(8,128)(2,1)S(1)} all-gather(bf16[16,1024]{1,0:T(8,128)(2,1)S(1)} %convert_element_type.148), channel_id=3, replica_groups=mesh['seq'=8,'tp'=4] {'seq'}, dimensions={0}, use_global_device_ids=true | all-gather | bytes 294912 | tf_op jit(solution)/shard_map/all_gather | solution.py:13
  1159.8 6.2 copy.52
  1166.0 13.8 %fusion.10 = f32[1024,16,64]{2,1,0:T(8,128)} fusion(f32[16,16,1024]{1,0,2:T(8,128)} %copy.52, f32[64]{0:T(128)S(1)} %broadcast_add_fusion, f32[16,1024]{0,1:T(8,128)S(1)} %copy.46, f32[16,1024]{0,1:T(8,128)S(1)} %copy.45), kind=kOutput, calls=%fused_computation.29 | convolution fusion | flops 203423744 | bytes 5374208 | tf_op jit(solution)/shard_map/inc,bnc->bic/dot_general | solution.py:102
  1179.8 32.7 %add_bitcast_fusion = f32[16,64,1024]{1,0,2:T(8,128)} fusion(f32[1024,16,64]{2,1,0:T(8,128)} %fusion.10, bf16[16,64,1024]{1,0,2:T(8,128)(2,1)S(1)} %copy-done, f32[64,64,1024]{1,0,2:T(8,128)} %copy.48, pred[64,64]{1,0:T(8,128)(4,1)S(1)} %get-tuple-element.169, pred[64,64]{1,0:T(8,128)(4,1)S(1)} %get-tuple-element.170), kind=kOutput, calls=%fused_computation.28 | convolution fusion | flops 814743552 | bytes 27271168 | tf_op jit(solution)/shard_map/ijc,bjc->bic/dot_general | solution.py:85
  1212.5 6.8 copy.53
  1219.3 5.5 fusion.39
  (112 shorter events, 76.4 us)
Async XLA Ops:
  7.2 267.5 %all-gather.7.cloned.1.call-start = ((), (), s32[]{:S(2)}) async-start(), calls=%async_computation | async-start | bytes 10485760 | tf_op jit(solution)/shard_map/all_gather | solution.py:130
  8.0 9.4 collective-permute-start
  37.7 8.7 collective-permute-start.1
  47.3 2.7 copy-start.8
  211.9 3.1 copy-start.4
  214.0 187.7 %all-gather.9.cloned.1.call-start = ((), (), s32[]{:S(2)}) async-start(), calls=%async_computation.1 | async-start | bytes 9437184 | tf_op jit(solution)/shard_map/all_gather | solution.py:131
  214.8 265.8 %all-gather.11.cloned.1.call-start = ((), (), s32[]{:S(2)}) async-start(), calls=%async_computation.2 | async-start | bytes 10485760 | tf_op jit(solution)/shard_map/all_gather | solution.py:143
  217.6 204.7 %dynamic-slice-start = ((f32[4096]{0:T(1024)}, s32[]{:T(128)}), f32[1024]{0:T(1024)S(1)}, s32[]{:S(2)}) async-start(f32[4096]{0:T(1024)} %param.19, s32[]{:T(128)} %select_n.20), calls=%async_computation.4 | async-start | bytes 8704 | tf_op jit(solution)/shard_map/dynamic_slice | solution.py:141
  416.0 8.9 copy-start.2
  416.0 8.8 copy-start.6
  416.0 8.8 copy-start.7
  416.0 40.4 %copy-start.5 = (f32[7,3,1024]{2,0,1:T(8,128)S(1)}, f32[7,3,1024]{2,0,1:T(8,128)}, u32[]{:S(2)}) copy-start(f32[7,3,1024]{2,0,1:T(8,128)} %param.21) | copy-start | bytes 258052
  424.2 538.2 %all-gather.13.cloned.1.call-start = ((), (), s32[]{:S(2)}) async-start(), calls=%async_computation.3 | async-start | bytes 28311552 | tf_op jit(solution)/shard_map/all_gather | solution.py:144
  995.4 2.6 copy-start.3
  998.1 55.9 %collective-permute-start.2 = (bf16[6,3,1024]{2,0,1:T(8,128)(2,1)S(1)}, bf16[6,3,1024]{2,0,1:T(8,128)(2,1)S(1)}, u32[]{:S(2)}, u32[]{:S(2)}) collective-permute-start(bf16[6,3,1024]{2,0,1:T(8,128)(2,1)S(1)} %slice.164), channel_id=1, source_target_pairs={{0,4},{4,8},{8,12},{12,16},{16,20},{20,24},{24,28},{1,5},{5,9},{9,... | collective-permute-start | bytes 110600 | tf_op jit(solution)/shard_map/ppermute | solution.py:33
  1073.2 4.5 copy-start.1
  1166.0 13.8 %copy-start = (bf16[16,64,1024]{1,0,2:T(8,128)(2,1)S(1)}, bf16[16,64,1024]{1,0,2:T(8,128)(2,1)}, u32[]{:S(2)}) copy-start(bf16[16,64,1024]{1,0,2:T(8,128)(2,1)} %copy.49) | copy-start | bytes 6291460
Sparse Core Ops, SparseCore 0:
  214.1 60.4 all-gather.6
  276.7 124.9 all-gather.8
  424.3 56.2 all-gather.10
  482.0 480.4 all-gather.12
where the time goes:
time: 1240 us; the launch traced here: 1230 us
  waiting for transfers between devices  684 us (55%)
  matrix products  264 us (21%)
  local copies, waits for them, and re-layouts  98.7 us (8%)
  other arithmetic  90.5 us (7%)
  blocking collectives  68.3 us (6%)
  between operations  14.4 us (1%)
    all_gather x1, waiting for transfers between devices, per_device(): pieces = lax.all_gather(lr_in, 'seq', axis=0, tiled=True)  482 us
    conv_general_dilated x1, matrix products, depthwise(): lax.conv_general_dilated(extended[None], flipped, (1,), [(0, 0)], dimensi...  159 us
    all_gather x1, waiting for transfers between devices, per_device(): pieces = lax.all_gather(mr_out, 'seq', axis=0, tiled=True)  127 us
    all_gather x2, blocking collectives, entering_2(): lax.all_gather(a.astype(kind), axis)  62 us
    all_gather x1, waiting for transfers between devices, per_device(): mixed = lax.all_gather(mr_gated, 'tp', axis=1, tiled=True)  57 us
    gather x2, local copies, waits for them, and re-layouts, lr_tables(): jnp.take(filter_lags, jnp.maximum(spread, 0), axis=0)  49 us
    add x2, other arithmetic, featurize(): total + taps[tap_index] * extended[begin:begin + row_count].astype(jnp.fl...  38.7 us
    dot_general x1, matrix products, per_device(): jnp.einsum('tm,mgc->tgc', columns, pieces, preferred_element_type=jnp.flo...  33 us
  transfers between devices with their start and end apart: 7, of which 5 were waited for; matrix products, arithmetic and copies ran while one was open for 6% of the time, Pallas kernels for 0%

commit v1 on v0

v1 whole, which is shorter than its diff:
```python
import functools

import jax
import jax.numpy as jnp
from jax import lax
from jax.experimental import pallas as pl
from jax.experimental.pallas import tpu as pltpu
from jax.sharding import PartitionSpec as P

norm_eps = 1e-06
LANES = 128
SUBS = 8
MR_HALO = 144
LR_HALO = 16
CHUNK = 256
STEP = 8
TILE = 16
MIB = 1024 * 1024


def ring_order(count):
    wide = 4 if count % 16 == 0 else 2
    high = count // wide
    order = [z * wide for z in range(high)]
    for turn, z in enumerate(reversed(range(high))):
        cells = range(1, wide) if turn % 2 == 0 else range(wide - 1, 0, -1)
        order += [z * wide + x for x in cells]
    return order


def featurize(ref, weights, first, sub):
    width = len(weights)
    window = [
        ref[pl.ds(first - (width - 1) + i, SUBS, stride=sub), :] for i in range(STEP + width - 1)
    ]
    out = []
    for i in range(STEP):
        total = weights[0] * window[i + width - 1]
        for j in range(1, width):
            total = total + weights[j] * window[i + width - 1 - j]
        out.append(total)
    return out


def spread(row):
    return jnp.broadcast_to(row, (SUBS, row.shape[-1]))


def mr_kernel(halo_ref, x_ref, short_ref, filter_ref, out_ref, xf, ue, qs, of, ff):
    rows = x_ref.shape[1]
    sub = rows // SUBS
    taps = short_ref.shape[1]
    length = filter_ref.shape[0]
    for g in range(3):
        xf[g, :MR_HALO, :] = halo_ref[g].astype(jnp.float32)
        xf[g, MR_HALO:, :] = x_ref[g].astype(jnp.float32)
    ff[...] = filter_ref[...].astype(jnp.float32)
    weights = [[spread(short_ref[g, pl.ds(j, 1), :]) for j in range(taps)] for g in range(3)]

    def products(step, _):
        first = MR_HALO - sub + step * STEP
        keys = featurize(xf.at[1], weights[1], first, sub)
        values = featurize(xf.at[2], weights[2], first, sub)
        for i in range(STEP):
            ue[step * STEP + i] = (keys[i] * values[i]).astype(jnp.bfloat16).astype(jnp.float32)
        return 0

    lax.fori_loop(0, 2 * sub // STEP, products, 0)

    def queries(step, _):
        found = featurize(xf.at[0], weights[0], MR_HALO + step * STEP, sub)
        for i in range(STEP):
            qs[step * STEP + i] = found[i]
        return 0

    lax.fori_loop(0, sub // STEP, queries, 0)

    def conv(tile, _):
        base = tile * TILE

        def taps_of(part, acc):
            acc = list(acc)
            start = sub + base - part * TILE - (TILE - 1)
            window = [ue[start + m] for m in range(2 * TILE - 1)]
            for j in range(TILE):
                weight = spread(ff[pl.ds(part * TILE + j, 1), :])
                for i in range(TILE):
                    acc[i] = acc[i] + weight * window[i - j + TILE - 1]
            return tuple(acc)

        zero = jnp.zeros((SUBS, LANES), jnp.float32)
        acc = lax.fori_loop(0, length // TILE, taps_of, (zero,) * TILE)
        for i in range(TILE):
            of[pl.ds(base + i, SUBS, stride=sub), :] = acc[i] * qs[base + i]
        return 0

    lax.fori_loop(0, sub // TILE, conv, 0)
    out_ref[...] = of[...].astype(jnp.bfloat16)


def mr_operator(halo, x, short, filters, first, count):
    rows = x.shape[1]
    sub = rows // SUBS
    skip = first // LANES
    return pl.pallas_call(
        mr_kernel,
        grid=(count // LANES,),
        out_shape=jax.ShapeDtypeStruct((rows, count), jnp.bfloat16),
        in_specs=[
            pl.BlockSpec((3, MR_HALO, LANES), lambda i: (0, 0, i + skip)),
            pl.BlockSpec((3, rows, LANES), lambda i: (0, 0, i + skip)),
            pl.BlockSpec((3, short.shape[1], LANES), lambda i: (0, 0, i + skip)),
            pl.BlockSpec((filters.shape[0], LANES), lambda i: (0, i + skip)),
        ],
        out_specs=pl.BlockSpec((rows, LANES), lambda i: (0, i)),
        scratch_shapes=[
            pltpu.VMEM((3, MR_HALO + rows, LANES), jnp.float32),
            pltpu.VMEM((2 * sub, SUBS, LANES), jnp.float32),
            pltpu.VMEM((sub, SUBS, LANES), jnp.float32),
            pltpu.VMEM((rows, LANES), jnp.float32),
            pltpu.VMEM((filters.shape[0], LANES), jnp.float32),
        ],
        compiler_params=pltpu.CompilerParams(vmem_limit_bytes=24 * MIB),
        cost_estimate=pl.CostEstimate(
            flops=rows * count * 340, bytes_accessed=rows * count * 10, transcendentals=0
        ),
        name="mr_operator",
    )(halo, x, short, filters)


def project(cols_ref, a_ref, blocks, pick):
    total = None
    for k, block in enumerate(blocks):
        w = pick(block)
        cols = a_ref[:, pl.ds(pl.multiple_of(cols_ref[k], LANES), w.shape[0])]
        part = jnp.dot(cols, w, preferred_element_type=jnp.float32)
        total = part if total is None else total + part
    return total


def stream_kernel(n_pieces, n_blocks, cols_ref, resid_ref, *refs):
    pieces = refs[:n_pieces]
    blocks = refs[n_pieces : n_pieces + n_blocks]
    out_ref, gated, sems = refs[n_pieces + n_blocks :]
    copies = []
    at = 0
    for i, piece in enumerate(pieces):
        width = piece.shape[1]
        copies.append(pltpu.make_async_copy(piece, gated.at[:, pl.ds(at, width)], sems.at[i]))
        at += width
    for copy in copies:
        copy.start()
    out_ref[:LR_HALO, :] = jnp.zeros((LR_HALO, out_ref.shape[1]), out_ref.dtype)
    for copy in copies:
        copy.wait()

    def tile(i, _):
        lanes = pl.ds(pl.multiple_of(i * CHUNK, CHUNK), CHUNK)
        projected = project(cols_ref, gated, blocks, lambda b: b[:, lanes])
        total = resid_ref[:, lanes].astype(jnp.float32) + projected
        out_ref[LR_HALO:, lanes] = total.astype(jnp.bfloat16)
        return 0

    lax.fori_loop(0, out_ref.shape[1] // CHUNK, tile, 0)


def stream_rows(cols, resid, pieces, blocks):
    rows, channels = resid.shape
    depth = sum(p.shape[1] for p in pieces)
    vmem = pl.BlockSpec(memory_space=pltpu.VMEM)
    return pl.pallas_call(
        functools.partial(stream_kernel, len(pieces), len(blocks)),
        out_shape=jax.ShapeDtypeStruct((LR_HALO + rows, channels), jnp.bfloat16),
        in_specs=[pl.BlockSpec(memory_space=pltpu.SMEM), vmem]
        + [pl.BlockSpec(memory_space=pl.ANY)] * len(pieces)
        + [vmem] * len(blocks),
        out_specs=vmem,
        scratch_shapes=[
            pltpu.VMEM((rows, depth), jnp.bfloat16),
            pltpu.SemaphoreType.DMA((len(pieces),)),
        ],
        compiler_params=pltpu.CompilerParams(vmem_limit_bytes=44 * MIB),
        cost_estimate=pl.CostEstimate(
            flops=2 * rows * channels * depth, bytes_accessed=4 * rows * depth, transcendentals=0
        ),
        name="stream_rows",
    )(cols, resid, *pieces, *blocks)


def norm_kernel(n_pieces, gain_ref, *refs):
    pieces, out_ref = refs[:n_pieces], refs[n_pieces]
    values = [p[...].astype(jnp.float32) for p in pieces]
    squares = sum(jnp.sum(v * v, axis=1, keepdims=True) for v in values)
    scale = lax.rsqrt(squares / out_ref.shape[1] + norm_eps)
    width = pieces[0].shape[1]
    for i, v in enumerate(values):
        lanes = slice(i * width, (i + 1) * width)
        out_ref[:, lanes] = (v * scale * gain_ref[:, lanes]).astype(jnp.bfloat16)


def norm_rows(gain, pieces):
    rows, width = pieces[0].shape
    depth = width * len(pieces)
    block = 80
    return pl.pallas_call(
        functools.partial(norm_kernel, len(pieces)),
        grid=(rows // block,),
        out_shape=jax.ShapeDtypeStruct((rows, depth), jnp.bfloat16),
        in_specs=[pl.BlockSpec((1, depth), lambda i: (0, 0))]
        + [pl.BlockSpec((block, width), lambda i: (i, 0))] * len(pieces),
        out_specs=pl.BlockSpec((block, depth), lambda i: (i, 0)),
        compiler_params=pltpu.CompilerParams(vmem_limit_bytes=24 * MIB),
        cost_estimate=pl.CostEstimate(
            flops=6 * rows * depth, bytes_accessed=4 * rows * depth, transcendentals=rows
        ),
        name="norm_rows",
    )(gain, *pieces)


def shifted(value, steps):
    place = lax.broadcasted_iota(jnp.int32, value.shape, 0)
    return jnp.where(place >= steps, pltpu.roll(value, steps, 0), 0.0)


def lr_kernel(n_blocks, cols_ref, a_ref, short_ref, rate_ref, residue_ref, *refs):
    blocks = refs[:n_blocks]
    query_ref, local_ref, enter_ref, last_ref, xs, us = refs[n_blocks:]
    rows = a_ref.shape[0] - LR_HALO
    sub = rows // SUBS
    taps = short_ref.shape[1]
    states = rate_ref.shape[0]
    tiles = CHUNK // LANES

    def group(g, _):
        found = project(cols_ref, a_ref, blocks, lambda b: b[g])
        found = found.astype(jnp.bfloat16).astype(jnp.float32)
        for t in range(tiles):
            xs[g * tiles + t] = found[:, t * LANES : (t + 1) * LANES]
        return 0

    lax.fori_loop(0, 3, group, 0)
    for t in range(tiles):
        lanes = slice(t * LANES, (t + 1) * LANES)
        weights = [
            [spread(short_ref[g, pl.ds(j, 1), lanes]) for j in range(taps)] for g in range(3)
        ]

        def features(step, _):
            first = LR_HALO + step * STEP
            queries, keys, values = [
                featurize(xs.at[g * tiles + t], weights[g], first, sub) for g in range(3)
            ]
            for i in range(STEP):
                query_ref[step * STEP + i, :, lanes] = queries[i]
                us[step * STEP + i] = (keys[i] * values[i]).astype(jnp.bfloat16).astype(jnp.float32)
            return 0

        lax.fori_loop(0, sub // STEP, features, 0)
        rate = rate_ref[:, lanes]
        coef = residue_ref[:, lanes] * jnp.sqrt(2.0 * rate)
        decay = jnp.exp(-rate)
        decays = [spread(decay[n : n + 1]) for n in range(states)]
        coefs = [spread(coef[n : n + 1]) for n in range(states)]

        def advance(step, held):
            held = list(held)
            for i in range(4):
                u = us[step * 4 + i]
                terms = []
                for n in range(states):
                    held[n] = decays[n] * held[n] + u
                    terms.append(coefs[n] * held[n])
                while len(terms) > 1:
                    terms = [sum(terms[k : k + 2]) for k in range(0, len(terms), 2)]
                local_ref[step * 4 + i, :, lanes] = terms[0]
            return tuple(held)

        zero = jnp.zeros((SUBS, LANES), jnp.float32)
        held = lax.fori_loop(0, sub // 4, advance, (zero,) * states)
        for n in range(states):
            total = held[n]
            for steps in (1, 2, 4):
                total = total + spread(jnp.exp(-rate[n : n + 1] * (sub * steps))) * shifted(
                    total, steps
                )
            enter_ref[n, :, lanes] = shifted(total, 1)
            last_ref[n : n + 1, lanes] = total[SUBS - 1 : SUBS]


def lr_local(cols, a, short, rate, residue, blocks, first):
    rows = a.shape[0] - LR_HALO
    sub = rows // SUBS
    states = rate.shape[0]
    skip = first // CHUNK
    vmem = pl.BlockSpec(memory_space=pltpu.VMEM)
    depth = a.shape[1]
    return pl.pallas_call(
        functools.partial(lr_kernel, len(blocks)),
        grid=(1,),
        out_shape=(
            jax.ShapeDtypeStruct((sub, SUBS, CHUNK), jnp.float32),
            jax.ShapeDtypeStruct((sub, SUBS, CHUNK), jnp.float32),
            jax.ShapeDtypeStruct((states, SUBS, CHUNK), jnp.float32),
            jax.ShapeDtypeStruct((states, CHUNK), jnp.float32),
        ),
        in_specs=[
            pl.BlockSpec(memory_space=pltpu.SMEM),
            vmem,
            pl.BlockSpec((3, short.shape[1], CHUNK), lambda i: (0, 0, skip)),
            pl.BlockSpec((states, CHUNK), lambda i: (0, skip)),
            pl.BlockSpec((states, CHUNK), lambda i: (0, skip)),
        ]
        + [vmem] * len(blocks),
        out_specs=(vmem, vmem, vmem, vmem),
        scratch_shapes=[
            pltpu.VMEM((3 * (CHUNK // LANES), LR_HALO + rows, LANES), jnp.float32),
            pltpu.VMEM((sub, SUBS, LANES), jnp.float32),
        ],
        compiler_params=pltpu.CompilerParams(vmem_limit_bytes=44 * MIB),
        cost_estimate=pl.CostEstimate(
            flops=2 * rows * 3 * CHUNK * depth, bytes_accessed=4 * rows * depth, transcendentals=0
        ),
        name="lr_local",
    )(cols, a, short, rate, residue, *blocks)


def finish_kernel(n_last, rate_ref, residue_ref, query_ref, local_ref, enter_ref, *refs):
    lasts = refs[:n_last]
    out_ref, of = refs[n_last:]
    sub = query_ref.shape[0]
    rate = rate_ref[...]
    states = rate.shape[0]
    coef = residue_ref[...] * jnp.sqrt(2.0 * rate)
    decay = jnp.exp(-rate)
    device = jnp.exp(-rate * (sub * SUBS))
    incoming = lasts[n_last - 1][...]
    for k in reversed(range(n_last - 1)):
        incoming = incoming * device + lasts[k][...]
    place = lax.broadcasted_iota(jnp.int32, (SUBS, LANES), 0).astype(jnp.float32) * float(sub)
    decays = [spread(decay[n : n + 1]) for n in range(states)]
    held = []
    for n in range(states):
        entering = enter_ref[n] + jnp.exp(-rate[n : n + 1] * place) * incoming[n : n + 1]
        held.append(coef[n : n + 1] * entering)

    def advance(step, held):
        held = list(held)
        for i in range(4):
            r = step * 4 + i
            for n in range(states):
                held[n] = decays[n] * held[n]
            terms = held
            while len(terms) > 1:
                terms = [sum(terms[k : k + 2]) for k in range(0, len(terms), 2)]
            of[pl.ds(r, SUBS, stride=sub), :] = query_ref[r] * (local_ref[r] + terms[0])
        return tuple(held)

    lax.fori_loop(0, sub // 4, advance, tuple(held))
    out_ref[...] = of[...].astype(jnp.bfloat16)


def lr_finish(rate, residue, query, local, enter, lasts, first):
    sub = query.shape[0]
    states = rate.shape[0]
    skip = first // LANES
    return pl.pallas_call(
        functools.partial(finish_kernel, len(lasts)),
        grid=(CHUNK // LANES,),
        out_shape=jax.ShapeDtypeStruct((sub * SUBS, CHUNK), jnp.bfloat16),
        in_specs=[
            pl.BlockSpec((states, LANES), lambda i: (0, i + skip)),
            pl.BlockSpec((states, LANES), lambda i: (0, i + skip)),
            pl.BlockSpec((sub, SUBS, LANES), lambda i: (0, 0, i)),
            pl.BlockSpec((sub, SUBS, LANES), lambda i: (0, 0, i)),
            pl.BlockSpec((states, SUBS, LANES), lambda i: (0, 0, i)),
        ]
        + [pl.BlockSpec((states, LANES), lambda i: (0, i))] * len(lasts),
        out_specs=pl.BlockSpec((sub * SUBS, LANES), lambda i: (0, i)),
        scratch_shapes=[pltpu.VMEM((sub * SUBS, LANES), jnp.float32)],
        compiler_params=pltpu.CompilerParams(vmem_limit_bytes=24 * MIB),
        cost_estimate=pl.CostEstimate(
            flops=sub * SUBS * CHUNK * 40, bytes_accessed=sub * SUBS * CHUNK * 10, transcendentals=0
        ),
        name="lr_finish",
    )(rate, residue, query, local, enter, *lasts)


def after(values, ties):
    if not ties:
        return values
    return lax.optimization_barrier((values, ties))[0]


class Ring:
    def __init__(self, own, order):
        count = len(order)
        self.steps = count // 2
        self.right = [(order[i], order[(i + 1) % count]) for i in range(count)]
        self.left = [(b, a) for a, b in self.right]
        self.ahead, self.behind = [own], [own]

    def step(self, ties):
        k = len(self.ahead)
        a, b = self.ahead[-1], self.behind[-1]
        if k == self.steps:
            half = a.shape[-2] // 2
            a, b = a[..., :half, :], b[..., half:, :]
        a, b = after((a, b), ties)
        self.ahead.append(lax.ppermute(a, "seq", self.right))
        self.behind.append(lax.ppermute(b, "seq", self.left))
        return (self.ahead[-1], self.behind[-1])

    def blocks(self):
        return self.ahead + self.behind[1:]


def block_columns(order, depth, channels):
    count = len(order)
    block = depth // count
    place = lax.axis_index("seq")
    spot = jnp.asarray([order.index(i) for i in range(count)], jnp.int32)[place]
    table = jnp.asarray(order, jnp.int32)
    half = count // 2
    turns = list(range(half + 1)) + [-k for k in range(1, half + 1)]
    source = table[(spot - jnp.asarray(turns, jnp.int32)) % count]
    shift = jnp.asarray([0] * (2 * half) + [block // 2], jnp.int32)
    row = source * block + shift
    peer = jnp.bitwise_xor(row // channels, lax.axis_index("tp"))
    return peer * channels + row % channels


def tp_pieces(own, count):
    def swap(value, mask):
        return lax.ppermute(value, "tp", [(i, i ^ mask) for i in range(count)])

    pieces = [own, swap(own, 1)]
    for mask in range(2, count, 2):
        far = swap(own, mask)
        pieces += [far, swap(far, 1)]
    return pieces


def from_behind(value, steps):
    count = lax.axis_size("seq")
    return lax.ppermute(value, "seq", [(i, i + steps) for i in range(count - steps)])


def per_device(
    mr_qkv,
    residual_in,
    mr_short,
    mr_filter,
    mr_out,
    norm_gain,
    lr_in,
    lr_short,
    lr_rate,
    lr_residue,
):
    rows, _, channels = mr_qkv.shape
    n_seq, n_tp = lax.axis_size("seq"), lax.axis_size("tp")
    depth = channels * n_tp
    order = ring_order(n_seq)
    x = mr_qkv.transpose(1, 0, 2)
    short = mr_short.transpose(1, 0, 2)
    halo = from_behind(x[:, rows - MR_HALO :], 1)
    starts = list(range(0, channels, CHUNK))

    rings = [Ring(mr_out, order)]
    weights = lr_in.transpose(1, 0, 2)
    for first in starts:
        rings.append(Ring(weights[:, :, first : first + CHUNK], order))
    half = rings[0].steps // 2
    plan = [(0, k) for k in range(half)]
    for i in range(len(rings)):
        for k in range(half):
            plan.append((i, half + k))
            if i + 1 < len(rings):
                plan.append((i + 1, k))
    done = []
    for i, _ in plan:
        done.append(rings[i].step(done[-2] if len(done) >= 2 else ()))

    parts = [mr_operator(halo, x, short, mr_filter, first, CHUNK) for first in starts]
    shared = [tp_pieces(part, n_tp) for part in parts]
    pieces = [shared[i][m] for m in range(n_tp) for i in range(len(starts))]
    cols = block_columns(order, depth, channels)
    extended = stream_rows(cols, residual_in, pieces, rings[0].blocks())
    stream = extended[LR_HALO:]
    rim = from_behind(extended[rows:], 1)
    extended = lax.dynamic_update_slice(extended, rim, (0, 0))
    gains = norm_gain.reshape(n_tp, channels)
    peers = jnp.bitwise_xor(jnp.arange(n_tp, dtype=jnp.int32), lax.axis_index("tp"))
    gain = jnp.take(gains, peers, axis=0).reshape(1, depth)
    normed = norm_rows(gain, tp_pieces(extended, n_tp))

    lr_taps = lr_short.transpose(1, 0, 2)
    outs = []
    for i, first in enumerate(starts):
        query, local, enter, last = lr_local(
            cols, normed, lr_taps, lr_rate, lr_residue, rings[i + 1].blocks(), first
        )
        lasts = [from_behind(last, k) for k in range(1, n_seq)]
        outs.append(lr_finish(lr_rate, lr_residue, query, local, enter, lasts, first))
    return (stream, jnp.concatenate(outs, axis=1))


def solution(mesh):
    placed = (
        P("seq", None, "tp"),
        P("seq", "tp"),
        P(None, None, "tp"),
        P(None, "tp"),
        P("seq", "tp"),
        P(),
        P("seq", None, "tp"),
        P(None, None, "tp"),
        P(None, "tp"),
        P(None, "tp"),
    )
    return jax.shard_map(
        per_device,
        mesh=mesh,
        in_specs=placed,
        out_specs=(P("seq", "tp"), P("seq", "tp")),
        check_vma=False,
    )
```

time: 1240 us -> 564 us (0.45)
  waiting for transfers between devices: 684 us -> 223 us
  matrix products: 264 us -> 0 us
  Pallas kernels: 0 us -> 179 us
  starting transfers between devices: 11.6 us -> 110 us
  other arithmetic: 90.5 us -> 2.37 us
  blocking collectives: 68.3 us -> 0 us
  local copies, waits for them, and re-layouts: 98.7 us -> 46.1 us
  between operations: 14.4 us -> 1.83 us
    all_gather x4 -> x0, waiting for transfers between devices: 678 us -> none  [the longest x1 482 us: per_device(): pieces = lax.all_gather(lr_in, 'seq', axis=0, tiled=True)]
    ppermute x3 -> x85, waiting for transfers between devices: 4.35 us -> 223 us  [the longest x20 114 us: step(): self.ahead.append(lax.ppermute(a, 'seq', self.right))]
    pallas_call x0 -> x14, Pallas kernels: none -> 179 us  [the longest x4 72.8 us: lr_local(): pl.pallas_call(functools.partial(lr_kernel, len(blocks)), grid=(1,), out_...]
    conv_general_dilated x1 -> x0, matrix products: 159 us -> none  [depthwise(): lax.conv_general_dilated(extended[None], flipped, (1,), [(0, 0)], dimensi...]
    dot_general x5 -> x0, matrix products: 105 us -> none  [the longest x1 33 us: per_device(): jnp.einsum('tm,mgc->tgc', columns, pieces, preferred_element_type=jnp.flo...]
    ppermute x3 -> x85, starting transfers between devices: 11.2 us -> 110 us  [the longest x30 59.5 us: from_behind(): lax.ppermute(value, 'seq', [(i, i + steps) for i in range(count - steps)])]
    all_gather x2 -> x0, blocking collectives: 62 us -> none  [entering_2(): lax.all_gather(a.astype(kind), axis)]
    add x20 -> x1, other arithmetic: 54.1 us -> 0.02 us  [block_columns(): return peer * channels + row % channels]
  transfers between devices with their start and end apart: 7 -> 85, of which waited for: 5 -> 22; matrix products, arithmetic and copies ran while one was open for 6% -> 3% of each run, Pallas kernels for 0% -> 32%
where the time goes in v1:
time: 564 us; the launch traced here: 563 us
  waiting for transfers between devices  223 us (40%)
  Pallas kernels  179 us (32%)
  starting transfers between devices  110 us (20%)
  local copies, waits for them, and re-layouts  46.1 us (8%)
    ppermute x20, waiting for transfers between devices, step(): self.ahead.append(lax.ppermute(a, 'seq', self.right))  114 us
    pallas_call x4, Pallas kernels, lr_local(): pl.pallas_call(functools.partial(lr_kernel, len(blocks)), grid=(1,), out_...  72.8 us
    pallas_call x4, Pallas kernels, mr_operator(): pl.pallas_call(mr_kernel, grid=(count // LANES,), out_shape=jax.ShapeDtyp...  71.5 us
    ppermute x30, starting transfers between devices, from_behind(): lax.ppermute(value, 'seq', [(i, i + steps) for i in range(count - steps)])  59.5 us
    ppermute x20, waiting for transfers between devices, step(): self.behind.append(lax.ppermute(b, 'seq', self.left))  46.6 us
    ppermute x20, starting transfers between devices, step(): self.ahead.append(lax.ppermute(a, 'seq', self.right))  33.7 us
    ppermute x30, waiting for transfers between devices, from_behind(): lax.ppermute(value, 'seq', [(i, i + steps) for i in range(count - steps)])  32.2 us
    ppermute x15, waiting for transfers between devices, swap(): return lax.ppermute(value, 'tp', [(i, i ^ mask) for i in range(count)])  30.3 us
  transfers between devices with their start and end apart: 85, of which 22 were waited for; matrix products, arithmetic and copies ran while one was open for 3% of the time, Pallas kernels for 32%

profile of v1, /device:TPU:0, one launch (start us, length us, event | category | flops | bytes accessed | tf_op | source)
XLA Modules:
  0.0 562.7 jit_solution(12277461120062384789)
XLA Ops:
  3.7 23.3 %collective-permute-done.13.refs_17_ = bf16[512,1024]{1,0:T(8,128)(2,1)S(1)} collective-permute-done((bf16[512,1024]{1,0:T(8,128)(2,1)}, bf16[512,1024]{1,0:T(8,128)(2,1)S(1)}, u32[]{:S(2)}, u32[]{:S(2)}) %collective-permute-start.13) | collective-permute-done | bytes 1048608 | tf_op jit(solution)/shard_map/ppermute | solution.py:409
  37.4 32.1 %collective-permute-done.halo_ref = bf16[3,144,1024]{2,1,0:T(8,128)(2,1)S(1)} collective-permute-done((bf16[3,144,1024]{2,1,0:T(8,128)(2,1)S(1)}, bf16[3,144,1024]{2,1,0:T(8,128)(2,1)S(1)}, u32[]{:S(2)}, u32[]{:S(2)}) %collective-permute-start) | collective-permute-done | bytes 884768 | tf_op jit(solution)/shard_map/ppermute | solution.py:445
  69.6 17.9 %mr_operator.4.refs_0_ = bf16[1024,256]{1,0:T(8,128)(2,1)S(1)} custom-call(bf16[3,144,1024]{2,1,0:T(8,128)(2,1)S(1)} %collective-permute-done.halo_ref, bf16[3,1024,1024]{2,1,0:T(8,128)(2,1)S(1)} %bitcast.12, f32[3,7,1024]{2,1,0:T(8,128)S(1)} %bitcast.16, bf16[128,1024]{1,0:T(8,128)(2,1)S(1)} %copy-done.3), custom_call_target="tpu_custom_call" | custom-call | flops 89128960 | bytes 2621440 | tf_op jit(solution)/shard_map/mr_operator/pallas_call | solution.py:105
  92.5 17.9 %mr_operator.5.refs_1_ = bf16[1024,256]{1,0:T(8,128)(2,1)S(1)} custom-call(bf16[3,144,1024]{2,1,0:T(8,128)(2,1)S(1)} %collective-permute-done.halo_ref, bf16[3,1024,1024]{2,1,0:T(8,128)(2,1)S(1)} %bitcast.13, f32[3,7,1024]{2,1,0:T(8,128)S(1)} %bitcast.17, bf16[128,1024]{1,0:T(8,128)(2,1)S(1)} %copy-done.3), custom_call_target="tpu_custom_call" | custom-call | flops 89128960 | bytes 2621440 | tf_op jit(solution)/shard_map/mr_operator/pallas_call | solution.py:105
  113.1 11.4 %collective-permute-done.6.refs_9_ = bf16[1024,256]{1,0:T(8,128)(2,1)S(1)} collective-permute-done((bf16[1024,256]{1,0:T(8,128)(2,1)S(1)}, bf16[1024,256]{1,0:T(8,128)(2,1)S(1)}, u32[]{:S(2)}, u32[]{:S(2)}) %collective-permute-start.6) | collective-permute-done | bytes 524320 | tf_op jit(solution)/shard_map/ppermute | solution.py:434
  125.3 17.9 %mr_operator.6.refs_2_ = bf16[1024,256]{1,0:T(8,128)(2,1)S(1)} custom-call(bf16[3,144,1024]{2,1,0:T(8,128)(2,1)S(1)} %collective-permute-done.halo_ref, bf16[3,1024,1024]{2,1,0:T(8,128)(2,1)S(1)} %bitcast.14, f32[3,7,1024]{2,1,0:T(8,128)S(1)} %bitcast.18, bf16[128,1024]{1,0:T(8,128)(2,1)S(1)} %copy-done.3), custom_call_target="tpu_custom_call" | custom-call | flops 89128960 | bytes 2621440 | tf_op jit(solution)/shard_map/mr_operator/pallas_call | solution.py:105
  145.6 12.0 %collective-permute-done.7.refs_10_ = bf16[1024,256]{1,0:T(8,128)(2,1)S(1)} collective-permute-done((bf16[1024,256]{1,0:T(8,128)(2,1)S(1)}, bf16[1024,256]{1,0:T(8,128)(2,1)S(1)}, u32[]{:S(2)}, u32[]{:S(2)}) %collective-permute-start.7) | collective-permute-done | bytes 524320 | tf_op jit(solution)/shard_map/ppermute | solution.py:434
  157.6 17.9 %mr_operator.7.refs_3_ = bf16[1024,256]{1,0:T(8,128)(2,1)S(1)} custom-call(bf16[3,144,1024]{2,1,0:T(8,128)(2,1)S(1)} %collective-permute-done.halo_ref, bf16[3,1024,1024]{2,1,0:T(8,128)(2,1)S(1)} %bitcast.15, f32[3,7,1024]{2,1,0:T(8,128)S(1)} %bitcast.19, bf16[128,1024]{1,0:T(8,128)(2,1)S(1)} %copy-done.3), custom_call_target="tpu_custom_call" | custom-call | flops 89128960 | bytes 2621440 | tf_op jit(solution)/shard_map/mr_operator/pallas_call | solution.py:105
  196.2 9.6 %collective-permute-done.19.refs_20_ = bf16[256,1024]{1,0:T(8,128)(2,1)} collective-permute-done((bf16[256,1024]{1,0:T(8,128)(2,1)}, bf16[256,1024]{1,0:T(8,128)(2,1)}, u32[]{:S(2)}, u32[]{:S(2)}) %collective-permute-start.19) | collective-permute-done | bytes 524320 | tf_op jit(solution)/shard_map/ppermute | solution.py:409
  212.7 17.3 %stream_rows.1 = bf16[1040,1024]{1,0:T(8,128)(2,1)} custom-call(s32[9]{0:T(128)S(1)} %fusion.cols_ref, bf16[1024,1024]{1,0:T(8,128)(2,1)} %resid_ref.1, bf16[1024,256]{1,0:T(8,128)(2,1)S(1)} %mr_operator.4.refs_0_, bf16[1024,256]{1,0:T(8,128)(2,1)S(1)} %mr_operator.5.refs_1_, bf16[1024,256]{1,0:T(8,128)(2,1)S(1)} %mr_operator.6.refs_2_, ...), custom_call_target="tpu_custom_call" | custom-call | flops 8589934592 | bytes 16777216 | tf_op jit(solution)/shard_map/stream_rows/pallas_call | solution.py:171
  243.7 14.5 %collective-permute-done.42.refs_2_ = bf16[3,512,256]{2,1,0:T(8,128)(2,1)S(1)} collective-permute-done((bf16[3,512,256]{2,1,0:T(8,128)(2,1)S(1)}, bf16[3,512,256]{2,1,0:T(8,128)(2,1)S(1)}, u32[]{:S(2)}, u32[]{:S(2)}) %collective-permute-start.42) | collective-permute-done | bytes 786464 | tf_op jit(solution)/shard_map/ppermute | solution.py:409
  263.3 11.7 %collective-permute-done.29.refs_3_ = bf16[3,512,256]{2,1,0:T(8,128)(2,1)S(1)} collective-permute-done((bf16[3,512,256]{2,1,0:T(8,128)(2,1)}, bf16[3,512,256]{2,1,0:T(8,128)(2,1)S(1)}, u32[]{:S(2)}, u32[]{:S(2)}) %collective-permute-start.29) | collective-permute-done | bytes 786464 | tf_op jit(solution)/shard_map/ppermute | solution.py:409
  280.3 11.6 %collective-permute-done.55.refs_1_ = bf16[3,512,256]{2,1,0:T(8,128)(2,1)S(1)} collective-permute-done((bf16[3,512,256]{2,1,0:T(8,128)(2,1)S(1)}, bf16[3,512,256]{2,1,0:T(8,128)(2,1)S(1)}, u32[]{:S(2)}, u32[]{:S(2)}) %collective-permute-start.55) | collective-permute-done | bytes 786464 | tf_op jit(solution)/shard_map/ppermute | solution.py:409
  308.0 9.1 %collective-permute-done.57.refs_2_ = bf16[3,512,256]{2,1,0:T(8,128)(2,1)S(1)} collective-permute-done((bf16[3,512,256]{2,1,0:T(8,128)(2,1)S(1)}, bf16[3,512,256]{2,1,0:T(8,128)(2,1)S(1)}, u32[]{:S(2)}, u32[]{:S(2)}) %collective-permute-start.57) | collective-permute-done | bytes 786464 | tf_op jit(solution)/shard_map/ppermute | solution.py:409
  322.0 12.1 %collective-permute-done.44.refs_3_ = bf16[3,512,256]{2,1,0:T(8,128)(2,1)S(1)} collective-permute-done((bf16[3,512,256]{2,1,0:T(8,128)(2,1)S(1)}, bf16[3,512,256]{2,1,0:T(8,128)(2,1)S(1)}, u32[]{:S(2)}, u32[]{:S(2)}) %collective-permute-start.44) | collective-permute-done | bytes 786464 | tf_op jit(solution)/shard_map/ppermute | solution.py:409
  336.4 20.2 %collective-permute-done.46.refs_4_ = bf16[3,256,256]{2,1,0:T(8,128)(2,1)S(1)} collective-permute-done((bf16[3,256,256]{2,1,0:T(8,128)(2,1)S(1)}, bf16[3,256,256]{2,1,0:T(8,128)(2,1)S(1)}, u32[]{:S(2)}, u32[]{:S(2)}) %collective-permute-start.46) | collective-permute-done | bytes 393248 | tf_op jit(solution)/shard_map/ppermute | solution.py:409
  363.7 14.2 %collective-permute-done.71.refs_5_ = bf16[3,512,256]{2,1,0:T(8,128)(2,1)} collective-permute-done((bf16[3,512,256]{2,1,0:T(8,128)(2,1)S(1)}, bf16[3,512,256]{2,1,0:T(8,128)(2,1)}, u32[]{:S(2)}, u32[]{:S(2)}) %collective-permute-start.71) | collective-permute-done | bytes 786464 | tf_op jit(solution)/shard_map/ppermute | solution.py:410
  381.6 13.1 %collective-permute-done.60.refs_7_ = bf16[3,512,256]{2,1,0:T(8,128)(2,1)S(1)} collective-permute-done((bf16[3,512,256]{2,1,0:T(8,128)(2,1)S(1)}, bf16[3,512,256]{2,1,0:T(8,128)(2,1)S(1)}, u32[]{:S(2)}, u32[]{:S(2)}) %collective-permute-start.60) | collective-permute-done | bytes 786464 | tf_op jit(solution)/shard_map/ppermute | solution.py:410
  401.3 9.4 %norm_rows.1.a_ref = bf16[1040,4096]{1,0:T(8,128)(2,1)S(1)} custom-call(f32[1,4096]{1,0:T(1,128)S(1)} %bitcast.20, bf16[1040,1024]{1,0:T(8,128)(2,1)S(1)} %constant_dynamic-update-slice_fusion.refs_0_, bf16[1040,1024]{1,0:T(8,128)(2,1)S(1)} %copy-done.5, bf16[1040,1024]{1,0:T(8,128)(2,1)} %collective-permute-done.23.refs_2_, ...), custom_call_target="tpu_custom_call" | custom-call | flops 25559040 | bytes 17039360 | tf_op jit(solution)/shard_map/norm_rows/pallas_call | solution.py:205
  421.0 18.6 %lr_local.4 = (f32[128,8,256]{2,1,0:T(8,128)S(1)}, f32[128,8,256]{2,1,0:T(8,128)S(1)}, f32[16,8,256]{2,1,0:T(8,128)S(1)}, f32[16,256]{1,0:T(8,128)S(1)}) custom-call(s32[9]{0:T(128)S(1)} %fusion.cols_ref, bf16[1040,4096]{1,0:T(8,128)(2,1)} %copy-done.2, f32[3,7,1024]{2,1,0:T(8,128)S(1)} %bitcast.21, f32[16,1024]{1,0:T(8,128)S(1)} %copy-done.7, ...), custom_call_target="tpu_custom_call" | custom-call | flops 6442450944 | bytes 16777216 | tf_op jit(solution)/shard_map/lr_local/pallas_call | solution.py:297
  447.8 6.9 %collective-permute-start.35 = (f32[16,256]{1,0:T(8,128)S(1)}, f32[16,256]{1,0:T(8,128)S(1)}, u32[]{:S(2)}, u32[]{:S(2)}) collective-permute-start(f32[16,256]{1,0:T(8,128)S(1)} %get-tuple-element.69), channel_id=1, source_target_pairs={{0,12},{4,16},{8,20},{12,24},{16,28},{1,13},{5,17},{9,21},{13,25},... | collective-permute-start | bytes 49160 | tf_op jit(solution)/shard_map/ppermute | solution.py:445
  457.0 17.9 %lr_local.5 = (f32[128,8,256]{2,1,0:T(8,128)S(1)}, f32[128,8,256]{2,1,0:T(8,128)S(1)}, f32[16,8,256]{2,1,0:T(8,128)S(1)}, f32[16,256]{1,0:T(8,128)S(1)}) custom-call(s32[9]{0:T(128)S(1)} %fusion.cols_ref, bf16[1040,4096]{1,0:T(8,128)(2,1)} %copy-done.2, f32[3,7,1024]{2,1,0:T(8,128)S(1)} %bitcast.22, f32[16,1024]{1,0:T(8,128)S(1)} %copy-done.7, ...), custom_call_target="tpu_custom_call" | custom-call | flops 6442450944 | bytes 16777216 | tf_op jit(solution)/shard_map/lr_local/pallas_call | solution.py:297
  489.4 17.8 %lr_local.6 = (f32[128,8,256]{2,1,0:T(8,128)S(1)}, f32[128,8,256]{2,1,0:T(8,128)S(1)}, f32[16,8,256]{2,1,0:T(8,128)S(1)}, f32[16,256]{1,0:T(8,128)S(1)}) custom-call(s32[9]{0:T(128)S(1)} %fusion.cols_ref, bf16[1040,4096]{1,0:T(8,128)(2,1)} %copy-done.2, f32[3,7,1024]{2,1,0:T(8,128)S(1)} %bitcast.23, f32[16,1024]{1,0:T(8,128)S(1)} %copy-done.7, ...), custom_call_target="tpu_custom_call" | custom-call | flops 6442450944 | bytes 16777216 | tf_op jit(solution)/shard_map/lr_local/pallas_call | solution.py:297
  516.8 18.5 %lr_local.7 = (f32[128,8,256]{2,1,0:T(8,128)S(1)}, f32[128,8,256]{2,1,0:T(8,128)S(1)}, f32[16,8,256]{2,1,0:T(8,128)S(1)}, f32[16,256]{1,0:T(8,128)S(1)}) custom-call(s32[9]{0:T(128)S(1)} %fusion.cols_ref, bf16[1040,4096]{1,0:T(8,128)(2,1)} %copy-done.2, f32[3,7,1024]{2,1,0:T(8,128)S(1)} %bitcast.24, f32[16,1024]{1,0:T(8,128)S(1)} %copy-done.7, ...), custom_call_target="tpu_custom_call" | custom-call | flops 6442450944 | bytes 16777216 | tf_op jit(solution)/shard_map/lr_local/pallas_call | solution.py:297
  (330 shorter events, 188.2 us)
Async XLA Ops:
  27.0 62.0 %collective-permute-start.14 = (bf16[512,1024]{1,0:T(8,128)(2,1)S(1)}, bf16[512,1024]{1,0:T(8,128)(2,1)S(1)}, u32[]{:S(2)}, u32[]{:S(2)}) collective-permute-start(bf16[512,1024]{1,0:T(8,128)(2,1)S(1)} %collective-permute-done.13.refs_17_), channel_id=1, source_target_pairs={{0,8},{8,16},{16,24},{24,28},{28,20},{20,12},{12,4},{4,0},{1,9},{9... | collective-permute-start | bytes 3145736 | tf_op jit(solution)/shard_map/ppermute | solution.py:409
  28.8 60.2 %collective-permute-start.16 = (bf16[512,1024]{1,0:T(8,128)(2,1)S(1)}, bf16[512,1024]{1,0:T(8,128)(2,1)S(1)}, u32[]{:S(2)}, u32[]{:S(2)}) collective-permute-start(bf16[512,1024]{1,0:T(8,128)(2,1)S(1)} %collective-permute-done.15.refs_21_), channel_id=1, source_target_pairs={{8,0},{16,8},{24,16},{28,24},{20,28},{12,20},{4,12},{0,4},{9,1},{1... | collective-permute-start | bytes 3145736 | tf_op jit(solution)/shard_map/ppermute | solution.py:410
  30.4 39.1 %collective-permute-start = (bf16[3,144,1024]{2,1,0:T(8,128)(2,1)S(1)}, bf16[3,144,1024]{2,1,0:T(8,128)(2,1)S(1)}, u32[]{:S(2)}, u32[]{:S(2)}) collective-permute-start(bf16[3,144,1024]{2,1,0:T(8,128)(2,1)S(1)} %slice.72), channel_id=1, source_target_pairs={{0,4},{4,8},{8,12},{12,16},{16,20},{20,24},{24,28},{1,5},{5,9},{9,... | collective-permute-start | bytes 2654216 | tf_op jit(solution)/shard_map/ppermute | solution.py:445
  89.0 54.2 %collective-permute-start.25 = (bf16[3,512,256]{2,1,0:T(8,128)(2,1)S(1)}, bf16[3,512,256]{2,1,0:T(8,128)(2,1)}, u32[]{:S(2)}, u32[]{:S(2)}) collective-permute-start(bf16[3,512,256]{2,1,0:T(8,128)(2,1)S(1)} %get-tuple-element.59.refs_0_), channel_id=1, source_target_pairs={{0,8},{8,16},{16,24},{24,28},{28,20},{20,12},{12,4},{4,0},{1,9},{9... | collective-permute-start | bytes 2359304 | tf_op jit(solution)/shard_map/ppermute | solution.py:409
  110.9 32.8 %collective-permute-start.26 = (bf16[3,512,256]{2,1,0:T(8,128)(2,1)S(1)}, bf16[3,512,256]{2,1,0:T(8,128)(2,1)}, u32[]{:S(2)}, u32[]{:S(2)}) collective-permute-start(bf16[3,512,256]{2,1,0:T(8,128)(2,1)S(1)} %get-tuple-element.59.refs_0_), channel_id=1, source_target_pairs={{8,0},{16,8},{24,16},{28,24},{20,28},{12,20},{4,12},{0,4},{9,1},{1... | collective-permute-start | bytes 2359304 | tf_op jit(solution)/shard_map/ppermute | solution.py:410
  110.9 65.9 %collective-permute-start.17 = (bf16[512,1024]{1,0:T(8,128)(2,1)S(1)}, bf16[512,1024]{1,0:T(8,128)(2,1)S(1)}, u32[]{:S(2)}, u32[]{:S(2)}) collective-permute-start(bf16[512,1024]{1,0:T(8,128)(2,1)S(1)} %collective-permute-done.14.refs_18_), channel_id=1, source_target_pairs={{0,8},{8,16},{16,24},{24,28},{28,20},{20,12},{12,4},{4,0},{1,9},{9... | collective-permute-start | bytes 3145736 | tf_op jit(solution)/shard_map/ppermute | solution.py:409
  113.0 64.8 %collective-permute-start.18 = (bf16[512,1024]{1,0:T(8,128)(2,1)S(1)}, bf16[512,1024]{1,0:T(8,128)(2,1)S(1)}, u32[]{:S(2)}, u32[]{:S(2)}) collective-permute-start(bf16[512,1024]{1,0:T(8,128)(2,1)S(1)} %collective-permute-done.16.refs_22_), channel_id=1, source_target_pairs={{8,0},{16,8},{24,16},{28,24},{20,28},{12,20},{4,12},{0,4},{9,1},{1... | collective-permute-start | bytes 3145736 | tf_op jit(solution)/shard_map/ppermute | solution.py:410
  143.8 31.8 %collective-permute-start.3 = (bf16[1024,256]{1,0:T(8,128)(2,1)S(1)}, bf16[1024,256]{1,0:T(8,128)(2,1)S(1)}, u32[]{:S(2)}, u32[]{:S(2)}) collective-permute-start(bf16[1024,256]{1,0:T(8,128)(2,1)S(1)} %mr_operator.6.refs_2_), channel_id=1, source_target_pairs={{0,1},{1,0},{2,3},{3,2},{4,5},{5,4},{6,7},{7,6},{8,9},{9,8},{10,11... | collective-permute-start | bytes 1572872 | tf_op jit(solution)/shard_map/ppermute | solution.py:434
  144.0 46.7 %collective-permute-start.27 = (bf16[3,512,256]{2,1,0:T(8,128)(2,1)}, bf16[3,512,256]{2,1,0:T(8,128)(2,1)}, u32[]{:S(2)}, u32[]{:S(2)}) collective-permute-start(bf16[3,512,256]{2,1,0:T(8,128)(2,1)} %collective-permute-done.25.refs_1_), channel_id=1, source_target_pairs={{0,8},{8,16},{16,24},{24,28},{28,20},{20,12},{12,4},{4,0},{1,9},{9... | collective-permute-start | bytes 2359304 | tf_op jit(solution)/shard_map/ppermute | solution.py:409
  157.6 34.8 %collective-permute-start.28 = (bf16[3,512,256]{2,1,0:T(8,128)(2,1)}, bf16[3,512,256]{2,1,0:T(8,128)(2,1)}, u32[]{:S(2)}, u32[]{:S(2)}) collective-permute-start(bf16[3,512,256]{2,1,0:T(8,128)(2,1)} %collective-permute-done.26.refs_5_), channel_id=1, source_target_pairs={{8,0},{16,8},{24,16},{28,24},{20,28},{12,20},{4,12},{0,4},{9,1},{1... | collective-permute-start | bytes 2359304 | tf_op jit(solution)/shard_map/ppermute | solution.py:410
  194.1 42.9 %collective-permute-start.40 = (bf16[3,512,256]{2,1,0:T(8,128)(2,1)}, bf16[3,512,256]{2,1,0:T(8,128)(2,1)S(1)}, u32[]{:S(2)}, u32[]{:S(2)}) collective-permute-start(bf16[3,512,256]{2,1,0:T(8,128)(2,1)} %get-tuple-element.71.refs_0_), channel_id=1, source_target_pairs={{0,8},{8,16},{16,24},{24,28},{28,20},{20,12},{12,4},{4,0},{1,9},{9... | collective-permute-start | bytes 2359304 | tf_op jit(solution)/shard_map/ppermute | solution.py:409
  195.9 41.1 %collective-permute-start.41 = (bf16[3,512,256]{2,1,0:T(8,128)(2,1)}, bf16[3,512,256]{2,1,0:T(8,128)(2,1)S(1)}, u32[]{:S(2)}, u32[]{:S(2)}) collective-permute-start(bf16[3,512,256]{2,1,0:T(8,128)(2,1)} %get-tuple-element.71.refs_0_), channel_id=1, source_target_pairs={{8,0},{16,8},{24,16},{28,24},{20,28},{12,20},{4,12},{0,4},{9,1},{1... | collective-permute-start | bytes 2359304 | tf_op jit(solution)/shard_map/ppermute | solution.py:410
  236.4 71.7 %collective-permute-start.23 = (bf16[1040,1024]{1,0:T(8,128)(2,1)S(1)}, bf16[1040,1024]{1,0:T(8,128)(2,1)}, u32[]{:S(2)}, u32[]{:S(2)}) collective-permute-start(bf16[1040,1024]{1,0:T(8,128)(2,1)S(1)} %constant_dynamic-update-slice_fusion.refs_0_), channel_id=1, source_target_pairs={{0,2},{1,3},{2,0},{3,1},{4,6},{5,7},{6,4},{7,5},{8,10},{9,11},{10,... | collective-permute-start | bytes 6389768 | tf_op jit(solution)/shard_map/ppermute | solution.py:434
  241.7 33.3 %collective-permute-start.29 = (bf16[3,512,256]{2,1,0:T(8,128)(2,1)}, bf16[3,512,256]{2,1,0:T(8,128)(2,1)S(1)}, u32[]{:S(2)}, u32[]{:S(2)}) collective-permute-start(bf16[3,512,256]{2,1,0:T(8,128)(2,1)} %collective-permute-done.27.refs_2_), channel_id=1, source_target_pairs={{0,8},{8,16},{16,24},{24,28},{28,20},{20,12},{12,4},{4,0},{1,9},{9... | collective-permute-start | bytes 2359304 | tf_op jit(solution)/shard_map/ppermute | solution.py:409
  243.7 34.4 %collective-permute-start.30 = (bf16[3,512,256]{2,1,0:T(8,128)(2,1)}, bf16[3,512,256]{2,1,0:T(8,128)(2,1)S(1)}, u32[]{:S(2)}, u32[]{:S(2)}) collective-permute-start(bf16[3,512,256]{2,1,0:T(8,128)(2,1)} %collective-permute-done.28.refs_6_), channel_id=1, source_target_pairs={{8,0},{16,8},{24,16},{28,24},{20,28},{12,20},{4,12},{0,4},{9,1},{1... | collective-permute-start | bytes 2359304 | tf_op jit(solution)/shard_map/ppermute | solution.py:410
  263.0 32.0 %collective-permute-start.56 = (bf16[3,512,256]{2,1,0:T(8,128)(2,1)S(1)}, bf16[3,512,256]{2,1,0:T(8,128)(2,1)S(1)}, u32[]{:S(2)}, u32[]{:S(2)}) collective-permute-start(bf16[3,512,256]{2,1,0:T(8,128)(2,1)S(1)} %copy-done.9), channel_id=1, source_target_pairs={{8,0},{16,8},{24,16},{28,24},{20,28},{12,20},{4,12},{0,4},{9,1},{1... | collective-permute-start | bytes 2359304 | tf_op jit(solution)/shard_map/ppermute | solution.py:410
  308.0 88.5 %collective-permute-start.22 = (bf16[1040,1024]{1,0:T(8,128)(2,1)S(1)}, bf16[1040,1024]{1,0:T(8,128)(2,1)S(1)}, u32[]{:S(2)}, u32[]{:S(2)}) collective-permute-start(bf16[1040,1024]{1,0:T(8,128)(2,1)S(1)} %constant_dynamic-update-slice_fusion.refs_0_), channel_id=1, source_target_pairs={{0,1},{1,0},{2,3},{3,2},{4,5},{5,4},{6,7},{7,6},{8,9},{9,8},{10,11... | collective-permute-start | bytes 6389768 | tf_op jit(solution)/shard_map/ppermute | solution.py:434
  317.2 82.5 %collective-permute-start.24 = (bf16[1040,1024]{1,0:T(8,128)(2,1)}, bf16[1040,1024]{1,0:T(8,128)(2,1)}, u32[]{:S(2)}, u32[]{:S(2)}) collective-permute-start(bf16[1040,1024]{1,0:T(8,128)(2,1)} %collective-permute-done.23.refs_2_), channel_id=1, source_target_pairs={{0,1},{1,0},{2,3},{3,2},{4,5},{5,4},{6,7},{7,6},{8,9},{9,8},{10,11... | collective-permute-start | bytes 6389768 | tf_op jit(solution)/shard_map/ppermute | solution.py:434
  320.3 40.7 %collective-permute-start.70 = (bf16[3,512,256]{2,1,0:T(8,128)(2,1)S(1)}, bf16[3,512,256]{2,1,0:T(8,128)(2,1)}, u32[]{:S(2)}, u32[]{:S(2)}) collective-permute-start(bf16[3,512,256]{2,1,0:T(8,128)(2,1)S(1)} %get-tuple-element.95.refs_0_), channel_id=1, source_target_pairs={{0,8},{8,16},{16,24},{24,28},{28,20},{20,12},{12,4},{4,0},{1,9},{9... | collective-permute-start | bytes 2359304 | tf_op jit(solution)/shard_map/ppermute | solution.py:409
  361.0 33.7 %collective-permute-start.60 = (bf16[3,512,256]{2,1,0:T(8,128)(2,1)S(1)}, bf16[3,512,256]{2,1,0:T(8,128)(2,1)S(1)}, u32[]{:S(2)}, u32[]{:S(2)}) collective-permute-start(bf16[3,512,256]{2,1,0:T(8,128)(2,1)S(1)} %collective-permute-done.58.refs_6_), channel_id=1, source_target_pairs={{8,0},{16,8},{24,16},{28,24},{20,28},{12,20},{4,12},{0,4},{9,1},{1... | collective-permute-start | bytes 2359304 | tf_op jit(solution)/shard_map/ppermute | solution.py:410
  377.9 39.0 %collective-permute-start.72 = (bf16[3,512,256]{2,1,0:T(8,128)(2,1)}, bf16[3,512,256]{2,1,0:T(8,128)(2,1)}, u32[]{:S(2)}, u32[]{:S(2)}) collective-permute-start(bf16[3,512,256]{2,1,0:T(8,128)(2,1)} %collective-permute-done.70.refs_1_), channel_id=1, source_target_pairs={{0,8},{8,16},{16,24},{24,28},{28,20},{20,12},{12,4},{4,0},{1,9},{9... | collective-permute-start | bytes 2359304 | tf_op jit(solution)/shard_map/ppermute | solution.py:409
  379.0 37.9 %collective-permute-start.73 = (bf16[3,512,256]{2,1,0:T(8,128)(2,1)}, bf16[3,512,256]{2,1,0:T(8,128)(2,1)}, u32[]{:S(2)}, u32[]{:S(2)}) collective-permute-start(bf16[3,512,256]{2,1,0:T(8,128)(2,1)} %collective-permute-done.71.refs_5_), channel_id=1, source_target_pairs={{8,0},{16,8},{24,16},{28,24},{20,28},{12,20},{4,12},{0,4},{9,1},{1... | collective-permute-start | bytes 2359304 | tf_op jit(solution)/shard_map/ppermute | solution.py:410
  416.9 63.8 %collective-permute-start.74 = (bf16[3,512,256]{2,1,0:T(8,128)(2,1)}, bf16[3,512,256]{2,1,0:T(8,128)(2,1)S(1)}, u32[]{:S(2)}, u32[]{:S(2)}) collective-permute-start(bf16[3,512,256]{2,1,0:T(8,128)(2,1)} %collective-permute-done.72.refs_2_), channel_id=1, source_target_pairs={{0,8},{8,16},{16,24},{24,28},{28,20},{20,12},{12,4},{4,0},{1,9},{9... | collective-permute-start | bytes 2359304 | tf_op jit(solution)/shard_map/ppermute | solution.py:409
  416.9 65.1 %collective-permute-start.75 = (bf16[3,512,256]{2,1,0:T(8,128)(2,1)}, bf16[3,512,256]{2,1,0:T(8,128)(2,1)S(1)}, u32[]{:S(2)}, u32[]{:S(2)}) collective-permute-start(bf16[3,512,256]{2,1,0:T(8,128)(2,1)} %collective-permute-done.73.refs_6_), channel_id=1, source_target_pairs={{8,0},{16,8},{24,16},{28,24},{20,28},{12,20},{4,12},{0,4},{9,1},{1... | collective-permute-start | bytes 2359304 | tf_op jit(solution)/shard_map/ppermute | solution.py:410
  (132 other events, 2518.9 us)

commit v2 on v1

--- a/solution.py
+++ b/solution.py
@@ -40,6 +40,10 @@
             total = total + weights[j] * window[i + width - 1 - j]
         out.append(total)
     return out
+
+
+def lasting(micros):
+    return pl.CostEstimate(flops=int(micros * 1.15e9), bytes_accessed=0, transcendentals=0)
 
 
 def spread(row):
@@ -121,9 +125,7 @@
             pltpu.VMEM((filters.shape[0], LANES), jnp.float32),
         ],
         compiler_params=pltpu.CompilerParams(vmem_limit_bytes=24 * MIB),
-        cost_estimate=pl.CostEstimate(
-            flops=rows * count * 340, bytes_accessed=rows * count * 10, transcendentals=0
-        ),
+        cost_estimate=lasting(rows * count * 6.8e-5),
         name="mr_operator",
     )(halo, x, short, filters)
 
@@ -180,9 +182,7 @@
             pltpu.SemaphoreType.DMA((len(pieces),)),
         ],
         compiler_params=pltpu.CompilerParams(vmem_limit_bytes=44 * MIB),
-        cost_estimate=pl.CostEstimate(
-            flops=2 * rows * channels * depth, bytes_accessed=4 * rows * depth, transcendentals=0
-        ),
+        cost_estimate=lasting(rows * channels * depth * 4e-9),
         name="stream_rows",
     )(cols, resid, *pieces, *blocks)
 
@@ -210,9 +210,7 @@
         + [pl.BlockSpec((block, width), lambda i: (i, 0))] * len(pieces),
         out_specs=pl.BlockSpec((block, depth), lambda i: (i, 0)),
         compiler_params=pltpu.CompilerParams(vmem_limit_bytes=24 * MIB),
-        cost_estimate=pl.CostEstimate(
-            flops=6 * rows * depth, bytes_accessed=4 * rows * depth, transcendentals=rows
-        ),
+        cost_estimate=lasting(rows * depth * 2.2e-6),
         name="norm_rows",
     )(gain, *pieces)
 
@@ -222,7 +220,7 @@
     return jnp.where(place >= steps, pltpu.roll(value, steps, 0), 0.0)
 
 
-def lr_kernel(n_blocks, cols_ref, a_ref, short_ref, rate_ref, residue_ref, *refs):
+def lr_kernel(n_blocks, part, cols_ref, a_ref, short_ref, rate_ref, residue_ref, *refs):
     blocks = refs[:n_blocks]
     query_ref, local_ref, enter_ref, last_ref, xs, us = refs[n_blocks:]
     rows = a_ref.shape[0] - LR_HALO
@@ -232,7 +230,9 @@
     tiles = CHUNK // LANES
 
     def group(g, _):
-        found = project(cols_ref, a_ref, blocks, lambda b: b[g])
+        found = project(
+            cols_ref, a_ref, blocks, lambda b: b[g, :, part * CHUNK : (part + 1) * CHUNK]
+        )
         found = found.astype(jnp.bfloat16).astype(jnp.float32)
         for t in range(tiles):
             xs[g * tiles + t] = found[:, t * LANES : (t + 1) * LANES]
@@ -287,15 +287,15 @@
             last_ref[n : n + 1, lanes] = total[SUBS - 1 : SUBS]
 
 
-def lr_local(cols, a, short, rate, residue, blocks, first):
+def lr_local(cols, a, short, rate, residue, blocks, first, part):
     rows = a.shape[0] - LR_HALO
     sub = rows // SUBS
     states = rate.shape[0]
-    skip = first // CHUNK
+    skip = first // CHUNK + part
     vmem = pl.BlockSpec(memory_space=pltpu.VMEM)
     depth = a.shape[1]
     return pl.pallas_call(
-        functools.partial(lr_kernel, len(blocks)),
+        functools.partial(lr_kernel, len(blocks), part),
         grid=(1,),
         out_shape=(
             jax.ShapeDtypeStruct((sub, SUBS, CHUNK), jnp.float32),
@@ -317,14 +317,12 @@
             pltpu.VMEM((sub, SUBS, LANES), jnp.float32),
         ],
         compiler_params=pltpu.CompilerParams(vmem_limit_bytes=44 * MIB),
-        cost_estimate=pl.CostEstimate(
-            flops=2 * rows * 3 * CHUNK * depth, bytes_accessed=4 * rows * depth, transcendentals=0
-        ),
+        cost_estimate=lasting(rows * CHUNK * depth * 1.7e-8),
         name="lr_local",
     )(cols, a, short, rate, residue, *blocks)
 
 
-def finish_kernel(n_last, rate_ref, residue_ref, query_ref, local_ref, enter_ref, *refs):
+def finish_kernel(n_last, odd_ref, rate_ref, residue_ref, query_ref, local_ref, enter_ref, *refs):
     lasts = refs[:n_last]
     out_ref, of = refs[n_last:]
     sub = query_ref.shape[0]
@@ -334,8 +332,9 @@
     decay = jnp.exp(-rate)
     device = jnp.exp(-rate * (sub * SUBS))
     incoming = lasts[n_last - 1][...]
-    for k in reversed(range(n_last - 1)):
-        incoming = incoming * device + lasts[k][...]
+    for k in reversed(range(1, n_last - 1)):
+        incoming = incoming * (device * device) + lasts[k][...]
+    incoming = jnp.where(odd_ref[0] == 1, incoming * device + lasts[0][...], incoming)
     place = lax.broadcasted_iota(jnp.int32, (SUBS, LANES), 0).astype(jnp.float32) * float(sub)
     decays = [spread(decay[n : n + 1]) for n in range(states)]
     held = []
@@ -359,30 +358,30 @@
     out_ref[...] = of[...].astype(jnp.bfloat16)
 
 
-def lr_finish(rate, residue, query, local, enter, lasts, first):
+def lr_finish(odd, rate, residue, query, local, enter, lasts, first, part):
     sub = query.shape[0]
     states = rate.shape[0]
-    skip = first // LANES
+    past = part * (CHUNK // LANES)
+    skip = first // LANES + past
     return pl.pallas_call(
         functools.partial(finish_kernel, len(lasts)),
         grid=(CHUNK // LANES,),
         out_shape=jax.ShapeDtypeStruct((sub * SUBS, CHUNK), jnp.bfloat16),
         in_specs=[
+            pl.BlockSpec(memory_space=pltpu.SMEM),
             pl.BlockSpec((states, LANES), lambda i: (0, i + skip)),
             pl.BlockSpec((states, LANES), lambda i: (0, i + skip)),
             pl.BlockSpec((sub, SUBS, LANES), lambda i: (0, 0, i)),
             pl.BlockSpec((sub, SUBS, LANES), lambda i: (0, 0, i)),
             pl.BlockSpec((states, SUBS, LANES), lambda i: (0, 0, i)),
         ]
-        + [pl.BlockSpec((states, LANES), lambda i: (0, i))] * len(lasts),
+        + [pl.BlockSpec((states, LANES), lambda i: (0, i + past))] * len(lasts),
         out_specs=pl.BlockSpec((sub * SUBS, LANES), lambda i: (0, i)),
         scratch_shapes=[pltpu.VMEM((sub * SUBS, LANES), jnp.float32)],
         compiler_params=pltpu.CompilerParams(vmem_limit_bytes=24 * MIB),
-        cost_estimate=pl.CostEstimate(
-            flops=sub * SUBS * CHUNK * 40, bytes_accessed=sub * SUBS * CHUNK * 10, transcendentals=0
-        ),
+        cost_estimate=lasting(sub * SUBS * CHUNK * 8e-6),
         name="lr_finish",
-    )(rate, residue, query, local, enter, *lasts)
+    )(odd, rate, residue, query, local, enter, *lasts)
 
 
 def after(values, ties):
@@ -429,20 +428,31 @@
     return peer * channels + row % channels
 
 
-def tp_pieces(own, count):
-    def swap(value, mask):
-        return lax.ppermute(value, "tp", [(i, i ^ mask) for i in range(count)])
-
-    pieces = [own, swap(own, 1)]
+def swap_tp(value, mask):
+    count = lax.axis_size("tp")
+    return lax.ppermute(value, "tp", [(i, i ^ mask) for i in range(count)])
+
+
+def tp_pieces(own, count, ties):
+    pieces = [own, swap_tp(own, 1)]
     for mask in range(2, count, 2):
-        far = swap(own, mask)
-        pieces += [far, swap(far, 1)]
+        far = swap_tp(own, mask)
+        pieces += [far, swap_tp(after(far, ties), 1)]
     return pieces
 
 
 def from_behind(value, steps):
     count = lax.axis_size("seq")
     return lax.ppermute(value, "seq", [(i, i + steps) for i in range(count - steps)])
+
+
+def earlier_states(last, rate, rows):
+    count = lax.axis_size("seq")
+    odd = lax.rem(lax.axis_index("seq"), 2)
+    other = lax.ppermute(last, "seq", [(i, i ^ 1) for i in range(count)])
+    first, second = jnp.where(odd == 1, other, last), jnp.where(odd == 1, last, other)
+    both = first * jnp.exp(-rate * rows) + second
+    return odd.reshape(1), other, [from_behind(both, 2 * k) for k in range(1, count // 2)]
 
 
 def per_device(
@@ -465,26 +475,64 @@
     short = mr_short.transpose(1, 0, 2)
     halo = from_behind(x[:, rows - MR_HALO :], 1)
     starts = list(range(0, channels, CHUNK))
+    final = len(starts)
+    wide = [2 * CHUNK] * (channels >= 4 * CHUNK)
+    wide += [CHUNK] * ((channels - sum(wide)) // CHUNK)
 
     rings = [Ring(mr_out, order)]
     weights = lr_in.transpose(1, 0, 2)
-    for first in starts:
-        rings.append(Ring(weights[:, :, first : first + CHUNK], order))
-    half = rings[0].steps // 2
-    plan = [(0, k) for k in range(half)]
-    for i in range(len(rings)):
-        for k in range(half):
-            plan.append((i, half + k))
-            if i + 1 < len(rings):
-                plan.append((i + 1, k))
+    first = 0
+    for width in wide:
+        rings.append(Ring(weights[:, :, first : first + width], order))
+        first += width
+    steps = rings[0].steps
+    begins = [0] + [steps - 1 + i * (steps - 2) for i in range(len(wide))]
+    plan = [
+        [(i, turn - begin) for i, begin in enumerate(begins) if 0 <= turn - begin < steps]
+        for turn in range(begins[-1] + steps)
+    ]
+    turns = len(plan)
+    waits = {}
     done = []
-    for i, _ in plan:
-        done.append(rings[i].step(done[-2] if len(done) >= 2 else ()))
-
-    parts = [mr_operator(halo, x, short, mr_filter, first, CHUNK) for first in starts]
-    shared = [tp_pieces(part, n_tp) for part in parts]
-    pieces = [shared[i][m] for m in range(n_tp) for i in range(len(starts))]
-    cols = block_columns(order, depth, channels)
+
+    def drive(turn):
+        while len(done) < min(turn, turns):
+            now = len(done)
+            ties = tuple(waits.get(now, ()))
+            got = []
+            for i, k in plan[now]:
+                fresh = k == 0 and now > 0
+                got += rings[i].step(ties + (tuple(done[-1][:2]) if fresh else ()))
+            done.append(got)
+        return tuple(done[min(turn, turns) - 1]) if turn > 0 else ()
+
+    def hold(turn, value):
+        waits.setdefault(turn + 1, []).append(value)
+
+    waits[0] = [halo]
+    parts, near, far, passed = [], [], [], []
+    for i, first in enumerate(starts):
+        ties = drive(i)
+        if i >= 2:
+            ties += tuple(far[i - 2])
+        if i >= 3:
+            ties += tuple(passed[i - 3])
+        parts.append(mr_operator(halo, x, after(short, ties), mr_filter, first, CHUNK))
+        hold(i, parts[-1])
+        if i > 0:
+            passed.append([swap_tp(after(f, [parts[i]]), 1) for f in far[i - 1]])
+        part = parts[-1] if i < final - 1 else after(parts[-1], drive(steps)[:2])
+        near.append(swap_tp(parts[-1], 1))
+        far.append([swap_tp(part, mask) for mask in range(2, n_tp, 2)])
+    passed.append([swap_tp(f, 1) for f in far[-1]])
+    pieces = []
+    for m in range(n_tp):
+        for i in range(final):
+            if m < 2:
+                pieces.append((parts, near)[m][i])
+            else:
+                pieces.append((far, passed)[m % 2][i][m // 2 - 1])
+    cols = after(block_columns(order, depth, channels), drive(steps))
     extended = stream_rows(cols, residual_in, pieces, rings[0].blocks())
     stream = extended[LR_HALO:]
     rim = from_behind(extended[rows:], 1)
@@ -492,16 +540,33 @@
     gains = norm_gain.reshape(n_tp, channels)
     peers = jnp.bitwise_xor(jnp.arange(n_tp, dtype=jnp.int32), lax.axis_index("tp"))
     gain = jnp.take(gains, peers, axis=0).reshape(1, depth)
-    normed = norm_rows(gain, tp_pieces(extended, n_tp))
+    shared = tp_pieces(extended, n_tp, drive(steps + 1))
+    turn = steps + 2
+    normed = norm_rows(after(gain, drive(turn)), shared)
+    hold(turn, normed)
 
     lr_taps = lr_short.transpose(1, 0, 2)
-    outs = []
-    for i, first in enumerate(starts):
-        query, local, enter, last = lr_local(
-            cols, normed, lr_taps, lr_rate, lr_residue, rings[i + 1].blocks(), first
-        )
-        lasts = [from_behind(last, k) for k in range(1, n_seq)]
-        outs.append(lr_finish(lr_rate, lr_residue, query, local, enter, lasts, first))
+    found = []
+    first = 0
+    for i, width in enumerate(wide):
+        turn = begins[i + 1] + steps - 1
+        drive(turn + 1)
+        taps = lr_taps
+        for part in range(width // CHUNK):
+            if part > 0:
+                taps = after(lr_taps, drive(turn + 1))
+            found.append(
+                lr_local(cols, normed, taps, lr_rate, lr_residue, rings[i + 1].blocks(), first, part)
+            )
+            hold(turn + 1, found[-1][3])
+        first += width
+    odd, other, fars = earlier_states(
+        jnp.concatenate([f[3] for f in found], axis=1), lr_rate, rows
+    )
+    outs = [
+        lr_finish(odd, lr_rate, lr_residue, query, local, enter, [other] + fars, 0, part)
+        for part, (query, local, enter, _) in enumerate(found)
+    ]
     return (stream, jnp.concatenate(outs, axis=1))
 
 

time: 564 us -> 444 us (0.79)
  waiting for transfers between devices: 223 us -> 161 us
  starting transfers between devices: 110 us -> 56.7 us
  local copies, waits for them, and re-layouts: 46.1 us -> 38.4 us
    ppermute x20 -> x16, waiting for transfers between devices: 114 us -> 61.7 us  [step(): self.ahead.append(lax.ppermute(a, 'seq', self.right))]
    ppermute x30 -> x5, starting transfers between devices: 59.5 us -> 15.7 us  [from_behind(): lax.ppermute(value, 'seq', [(i, i + steps) for i in range(count - steps)])]
    ppermute x20 -> x16, waiting for transfers between devices: 46.6 us -> 17.6 us  [step(): self.behind.append(lax.ppermute(b, 'seq', self.left))]
    ppermute x15 -> x16, waiting for transfers between devices: 30.3 us -> 56.8 us  [the longest x15 52.8 us: swap_tp(): return lax.ppermute(value, 'tp', [(i, i ^ mask) for i in range(count)])]
    ppermute x20 -> x16, starting transfers between devices: 33.7 us -> 16.4 us  [step(): self.ahead.append(lax.ppermute(a, 'seq', self.right))]
    ppermute x30 -> x5, waiting for transfers between devices: 32.2 us -> 24.5 us  [from_behind(): lax.ppermute(value, 'seq', [(i, i + steps) for i in range(count - steps)])]
    ppermute x20 -> x16, starting transfers between devices: 12.6 us -> 17.5 us  [step(): self.behind.append(lax.ppermute(b, 'seq', self.left))]
    unnamed x143 -> x126, local copies, waits for them, and re-layouts: 29.9 us -> 27.4 us
  transfers between devices with their start and end apart: 85 -> 53, of which waited for: 22 -> 24; matrix products, arithmetic and copies ran while one was open for 3% -> 2% of each run, Pallas kernels for 32% -> 33%
where the time goes in v2:
time: 444 us; the launch traced here: 443 us
  Pallas kernels  183 us (41%)
  waiting for transfers between devices  161 us (36%)
  starting transfers between devices  56.7 us (13%)
  local copies, waits for them, and re-layouts  38.4 us (9%)
    pallas_call x4, Pallas kernels, lr_local(): pl.pallas_call(functools.partial(lr_kernel, len(blocks), part), grid=(1,)...  75.5 us
    pallas_call x4, Pallas kernels, mr_operator(): pl.pallas_call(mr_kernel, grid=(count // LANES,), out_shape=jax.ShapeDtyp...  72.1 us
    ppermute x16, waiting for transfers between devices, step(): self.ahead.append(lax.ppermute(a, 'seq', self.right))  61.7 us
    ppermute x15, waiting for transfers between devices, swap_tp(): return lax.ppermute(value, 'tp', [(i, i ^ mask) for i in range(count)])  52.8 us
    unnamed x126, local copies, waits for them, and re-layouts  27.4 us
    ppermute x5, waiting for transfers between devices, from_behind(): lax.ppermute(value, 'seq', [(i, i + steps) for i in range(count - steps)])  24.5 us
    ppermute x16, waiting for transfers between devices, step(): self.behind.append(lax.ppermute(b, 'seq', self.left))  17.6 us
    ppermute x16, starting transfers between devices, step(): self.behind.append(lax.ppermute(b, 'seq', self.left))  17.5 us
  transfers between devices with their start and end apart: 53, of which 24 were waited for; matrix products, arithmetic and copies ran while one was open for 2% of the time, Pallas kernels for 33%

profile of v2, /device:TPU:0, one launch (start us, length us, event | category | flops | bytes accessed | tf_op | source)
XLA Modules:
  0.0 442.7 jit_solution(1053583793457893155)
XLA Ops:
  2.0 4.9 %collective-permute-start = (bf16[3,144,1024]{2,1,0:T(8,128)(2,1)S(1)}, bf16[3,144,1024]{2,1,0:T(8,128)(2,1)S(1)}, u32[]{:S(2)}, u32[]{:S(2)}) collective-permute-start(bf16[3,144,1024]{2,1,0:T(8,128)(2,1)S(1)} %slice.60), channel_id=1, source_target_pairs={{0,4},{4,8},{8,12},{12,16},{16,20},{20,24},{24,28},{1,5},{5,9},{9,... | collective-permute-start | bytes 2654216 | tf_op jit(solution)/shard_map/ppermute | solution.py:446
  8.4 17.3 %collective-permute-done.halo_ref = bf16[3,144,1024]{2,1,0:T(8,128)(2,1)S(1)} collective-permute-done((bf16[3,144,1024]{2,1,0:T(8,128)(2,1)S(1)}, bf16[3,144,1024]{2,1,0:T(8,128)(2,1)S(1)}, u32[]{:S(2)}, u32[]{:S(2)}) %collective-permute-start) | collective-permute-done | bytes 884768 | tf_op jit(solution)/shard_map/ppermute | solution.py:446
  32.0 17.9 %mr_operator.4.refs_0_ = bf16[1024,256]{1,0:T(8,128)(2,1)S(1)} custom-call(bf16[3,144,1024]{2,1,0:T(8,128)(2,1)S(1)} %collective-permute-done.halo_ref, bf16[3,1024,1024]{2,1,0:T(8,128)(2,1)S(1)} %bitcast.13, f32[3,7,1024]{2,1,0:T(8,128)S(1)} %bitcast.18, bf16[128,1024]{1,0:T(8,128)(2,1)S(1)} %copy-done.27), custom_call_target="tpu_custom_call" | custom-call | flops 20499660800 | tf_op jit(solution)/shard_map/mr_operator/pallas_call | solution.py:109
  55.0 17.9 %mr_operator.5.refs_1_ = bf16[1024,256]{1,0:T(8,128)(2,1)S(1)} custom-call(bf16[3,144,1024]{2,1,0:T(8,128)(2,1)S(1)} %collective-permute-done.halo_ref, bf16[3,1024,1024]{2,1,0:T(8,128)(2,1)S(1)} %bitcast.14, f32[3,7,1024]{2,1,0:T(8,128)S(1)} %bitcast.19, bf16[128,1024]{1,0:T(8,128)(2,1)S(1)} %copy-done.27), custom_call_target="tpu_custom_call" | custom-call | flops 20499660800 | tf_op jit(solution)/shard_map/mr_operator/pallas_call | solution.py:109
  79.1 17.9 %mr_operator.6.refs_2_ = bf16[1024,256]{1,0:T(8,128)(2,1)S(1)} custom-call(bf16[3,144,1024]{2,1,0:T(8,128)(2,1)S(1)} %collective-permute-done.halo_ref, bf16[3,1024,1024]{2,1,0:T(8,128)(2,1)S(1)} %bitcast.15, f32[3,7,1024]{2,1,0:T(8,128)S(1)} %bitcast.20, bf16[128,1024]{1,0:T(8,128)(2,1)S(1)} %copy-done.27), custom_call_target="tpu_custom_call" | custom-call | flops 20499660800 | tf_op jit(solution)/shard_map/mr_operator/pallas_call | solution.py:109
  105.7 18.5 %mr_operator.7.refs_3_ = bf16[1024,256]{1,0:T(8,128)(2,1)} custom-call(bf16[3,144,1024]{2,1,0:T(8,128)(2,1)S(1)} %collective-permute-done.halo_ref, bf16[3,1024,1024]{2,1,0:T(8,128)(2,1)S(1)} %bitcast.16, f32[3,7,1024]{2,1,0:T(8,128)S(1)} %bitcast.21, bf16[128,1024]{1,0:T(8,128)(2,1)S(1)} %copy-done.27), custom_call_target="tpu_custom_call" | custom-call | flops 20499660800 | tf_op jit(solution)/shard_map/mr_operator/pallas_call | solution.py:109
  128.8 12.4 %collective-permute-done.19.refs_11_ = bf16[1024,256]{1,0:T(8,128)(2,1)} collective-permute-done((bf16[1024,256]{1,0:T(8,128)(2,1)}, bf16[1024,256]{1,0:T(8,128)(2,1)}, u32[]{:S(2)}, u32[]{:S(2)}) %collective-permute-start.19) | collective-permute-done | bytes 524320 | tf_op jit(solution)/shard_map/ppermute | solution.py:433
  141.2 4.7 %collective-permute-done.10.refs_1_ = bf16[3,512,512]{2,1,0:T(8,128)(2,1)} collective-permute-done((bf16[3,512,512]{2,1,0:T(8,128)(2,1)S(1)}, bf16[3,512,512]{2,1,0:T(8,128)(2,1)}, u32[]{:S(2)}, u32[]{:S(2)}) %collective-permute-start.10) | collective-permute-done | bytes 1572896 | tf_op jit(solution)/shard_map/ppermute | solution.py:408
  157.6 17.2 %stream_rows.1 = bf16[1040,1024]{1,0:T(8,128)(2,1)} custom-call(s32[9]{0:T(128)S(1)} %fusion.cols_ref, bf16[1024,1024]{1,0:T(8,128)(2,1)} %resid_ref.1, bf16[1024,256]{1,0:T(8,128)(2,1)S(1)} %mr_operator.4.refs_0_, bf16[1024,256]{1,0:T(8,128)(2,1)S(1)} %mr_operator.5.refs_1_, bf16[1024,256]{1,0:T(8,128)(2,1)S(1)} %copy-done.20, ...), custom_call_target="tpu_custom_call" | custom-call | flops 19756849152 | tf_op jit(solution)/shard_map/stream_rows/pallas_call | solution.py:173
  181.0 5.3 %collective-permute-done.29 = bf16[16,1024]{1,0:T(8,128)(2,1)S(1)} collective-permute-done((bf16[16,1024]{1,0:T(8,128)(2,1)S(1)}, bf16[16,1024]{1,0:T(8,128)(2,1)S(1)}, u32[]{:S(2)}, u32[]{:S(2)}) %collective-permute-start.29) | collective-permute-done | bytes 32800 | tf_op jit(solution)/shard_map/ppermute | solution.py:446
  193.7 40.4 %collective-permute-done.31.refs_2_ = bf16[1040,1024]{1,0:T(8,128)(2,1)} collective-permute-done((bf16[1040,1024]{1,0:T(8,128)(2,1)S(1)}, bf16[1040,1024]{1,0:T(8,128)(2,1)}, u32[]{:S(2)}, u32[]{:S(2)}) %collective-permute-start.31) | collective-permute-done | bytes 2129952 | tf_op jit(solution)/shard_map/ppermute | solution.py:433
  234.6 7.7 %collective-permute-done.28.refs_5_ = bf16[3,512,256]{2,1,0:T(8,128)(2,1)} collective-permute-done((bf16[3,512,256]{2,1,0:T(8,128)(2,1)S(1)}, bf16[3,512,256]{2,1,0:T(8,128)(2,1)}, u32[]{:S(2)}, u32[]{:S(2)}) %collective-permute-start.28) | collective-permute-done | bytes 786464 | tf_op jit(solution)/shard_map/ppermute | solution.py:409
  247.9 14.9 %collective-permute-done.35.refs_2_ = bf16[3,512,256]{2,1,0:T(8,128)(2,1)S(1)} collective-permute-done((bf16[3,512,256]{2,1,0:T(8,128)(2,1)S(1)}, bf16[3,512,256]{2,1,0:T(8,128)(2,1)S(1)}, u32[]{:S(2)}, u32[]{:S(2)}) %collective-permute-start.35) | collective-permute-done | bytes 786464 | tf_op jit(solution)/shard_map/ppermute | solution.py:408
  265.9 10.8 %collective-permute-done.33.refs_4_ = bf16[3,256,512]{2,1,0:T(8,128)(2,1)} collective-permute-done((bf16[3,256,512]{2,1,0:T(8,128)(2,1)}, bf16[3,256,512]{2,1,0:T(8,128)(2,1)}, u32[]{:S(2)}, u32[]{:S(2)}) %collective-permute-start.33) | collective-permute-done | bytes 786464 | tf_op jit(solution)/shard_map/ppermute | solution.py:408
  277.6 10.0 %norm_rows.1.a_ref = bf16[1040,4096]{1,0:T(8,128)(2,1)S(1)} custom-call(f32[1,4096]{1,0:T(1,128)S(1)} %bitcast.17, bf16[1040,1024]{1,0:T(8,128)(2,1)S(1)} %constant_dynamic-update-slice_fusion.4.refs_0_, bf16[1040,1024]{1,0:T(8,128)(2,1)} %collective-permute-done.30.refs_1_, bf16[1040,1024]{1,0:T(8,128)(2,1)} %collective-permute-done.31.refs_2_, ...), custom_call_target="tpu_custom_call" | custom-call | flops 10777395200 | tf_op jit(solution)/shard_map/norm_rows/pallas_call | solution.py:205
  296.4 19.8 %lr_local.4 = (f32[128,8,256]{2,1,0:T(8,128)S(1)}, f32[128,8,256]{2,1,0:T(8,128)S(1)}, f32[16,8,256]{2,1,0:T(8,128)S(1)}, f32[16,256]{1,0:T(8,128)S(1)}) custom-call(s32[9]{0:T(128)S(1)} %fusion.cols_ref, bf16[1040,4096]{1,0:T(8,128)(2,1)} %copy-done.43, f32[3,7,1024]{2,1,0:T(8,128)S(1)} %bitcast.22, f32[16,1024]{1,0:T(8,128)S(1)} %copy-done.8, ...), custom_call_target="tpu_custom_call" | custom-call | flops 20991651840 | tf_op jit(solution)/shard_map/lr_local/pallas_call | solution.py:297
  316.3 19.9 %lr_local.5 = (f32[128,8,256]{2,1,0:T(8,128)S(1)}, f32[128,8,256]{2,1,0:T(8,128)S(1)}, f32[16,8,256]{2,1,0:T(8,128)S(1)}, f32[16,256]{1,0:T(8,128)S(1)}) custom-call(s32[9]{0:T(128)S(1)} %fusion.cols_ref, bf16[1040,4096]{1,0:T(8,128)(2,1)} %copy-done.43, f32[3,7,1024]{2,1,0:T(8,128)S(1)} %bitcast.23, f32[16,1024]{1,0:T(8,128)S(1)} %copy-done.8, ...), custom_call_target="tpu_custom_call" | custom-call | flops 20991651840 | tf_op jit(solution)/shard_map/lr_local/pallas_call | solution.py:297
  341.5 16.3 %collective-permute-done.43.refs_2_ = bf16[3,512,256]{2,1,0:T(8,128)(2,1)S(1)} collective-permute-done((bf16[3,512,256]{2,1,0:T(8,128)(2,1)S(1)}, bf16[3,512,256]{2,1,0:T(8,128)(2,1)S(1)}, u32[]{:S(2)}, u32[]{:S(2)}) %collective-permute-start.43) | collective-permute-done | bytes 786464 | tf_op jit(solution)/shard_map/ppermute | solution.py:408
  359.8 6.4 %collective-permute-done.39.refs_4_ = bf16[3,256,256]{2,1,0:T(8,128)(2,1)S(1)} collective-permute-done((bf16[3,256,256]{2,1,0:T(8,128)(2,1)S(1)}, bf16[3,256,256]{2,1,0:T(8,128)(2,1)S(1)}, u32[]{:S(2)}, u32[]{:S(2)}) %collective-permute-start.39) | collective-permute-done | bytes 393248 | tf_op jit(solution)/shard_map/ppermute | solution.py:408
  366.4 18.2 %lr_local.6 = (f32[128,8,256]{2,1,0:T(8,128)S(1)}, f32[128,8,256]{2,1,0:T(8,128)S(1)}, f32[16,8,256]{2,1,0:T(8,128)S(1)}, f32[16,256]{1,0:T(8,128)S(1)}) custom-call(s32[9]{0:T(128)S(1)} %fusion.cols_ref, bf16[1040,4096]{1,0:T(8,128)(2,1)} %copy-done.43, f32[3,7,1024]{2,1,0:T(8,128)S(1)} %bitcast.24, f32[16,1024]{1,0:T(8,128)S(1)} %copy-done.8, ...), custom_call_target="tpu_custom_call" | custom-call | flops 20991651840 | tf_op jit(solution)/shard_map/lr_local/pallas_call | solution.py:297
  386.7 5.7 %collective-permute-done.47.refs_4_ = bf16[3,256,256]{2,1,0:T(8,128)(2,1)S(1)} collective-permute-done((bf16[3,256,256]{2,1,0:T(8,128)(2,1)S(1)}, bf16[3,256,256]{2,1,0:T(8,128)(2,1)S(1)}, u32[]{:S(2)}, u32[]{:S(2)}) %collective-permute-start.47) | collective-permute-done | bytes 393248 | tf_op jit(solution)/shard_map/ppermute | solution.py:408
  394.2 17.6 %lr_local.7 = (f32[128,8,256]{2,1,0:T(8,128)S(1)}, f32[128,8,256]{2,1,0:T(8,128)S(1)}, f32[16,8,256]{2,1,0:T(8,128)S(1)}, f32[16,256]{1,0:T(8,128)S(1)}) custom-call(s32[9]{0:T(128)S(1)} %fusion.cols_ref, bf16[1040,4096]{1,0:T(8,128)(2,1)} %copy-done.43, f32[3,7,1024]{2,1,0:T(8,128)S(1)} %bitcast.25, f32[16,1024]{1,0:T(8,128)S(1)} %copy-done.8, ...), custom_call_target="tpu_custom_call" | custom-call | flops 20991651840 | tf_op jit(solution)/shard_map/lr_local/pallas_call | solution.py:297
  414.7 4.0 collective-permute-done.49.refs_0_
  422.3 3.8 collective-permute-start.51
  (249 shorter events, 111.9 us)
Async XLA Ops:
  25.7 25.7 %collective-permute-start.1 = (bf16[512,1024]{1,0:T(8,128)(2,1)S(1)}, bf16[512,1024]{1,0:T(8,128)(2,1)S(1)}, u32[]{:S(2)}, u32[]{:S(2)}) collective-permute-start(bf16[512,1024]{1,0:T(8,128)(2,1)S(1)} %copy-done.54), channel_id=1, source_target_pairs={{0,8},{8,16},{16,24},{24,28},{28,20},{20,12},{12,4},{4,0},{1,9},{9... | collective-permute-start | bytes 3145736 | tf_op jit(solution)/shard_map/ppermute | solution.py:408
  72.9 30.7 %collective-permute-start.12 = (bf16[1024,256]{1,0:T(8,128)(2,1)S(1)}, bf16[1024,256]{1,0:T(8,128)(2,1)S(1)}, u32[]{:S(2)}, u32[]{:S(2)}) collective-permute-start(bf16[1024,256]{1,0:T(8,128)(2,1)S(1)} %mr_operator.5.refs_1_), channel_id=1, source_target_pairs={{0,2},{1,3},{2,0},{3,1},{4,6},{5,7},{6,4},{7,5},{8,10},{9,11},{10,... | collective-permute-start | bytes 1572872 | tf_op jit(solution)/shard_map/ppermute | solution.py:433
  74.5 30.7 %collective-permute-start.13 = (bf16[1024,256]{1,0:T(8,128)(2,1)S(1)}, bf16[1024,256]{1,0:T(8,128)(2,1)S(1)}, u32[]{:S(2)}, u32[]{:S(2)}) collective-permute-start(bf16[1024,256]{1,0:T(8,128)(2,1)S(1)} %collective-permute-done.7.refs_8_), channel_id=1, source_target_pairs={{0,1},{1,0},{2,3},{3,2},{4,5},{5,4},{6,7},{7,6},{8,9},{9,8},{10,11... | collective-permute-start | bytes 1572872 | tf_op jit(solution)/shard_map/ppermute | solution.py:433
  97.0 29.3 %collective-permute-start.18 = (bf16[1024,256]{1,0:T(8,128)(2,1)S(1)}, bf16[1024,256]{1,0:T(8,128)(2,1)S(1)}, u32[]{:S(2)}, u32[]{:S(2)}) collective-permute-start(bf16[1024,256]{1,0:T(8,128)(2,1)S(1)} %mr_operator.6.refs_2_), channel_id=1, source_target_pairs={{0,2},{1,3},{2,0},{3,1},{4,6},{5,7},{6,4},{7,5},{8,10},{9,11},{10,... | collective-permute-start | bytes 1572872 | tf_op jit(solution)/shard_map/ppermute | solution.py:433
  103.6 42.4 %collective-permute-start.10 = (bf16[3,512,512]{2,1,0:T(8,128)(2,1)S(1)}, bf16[3,512,512]{2,1,0:T(8,128)(2,1)}, u32[]{:S(2)}, u32[]{:S(2)}) collective-permute-start(bf16[3,512,512]{2,1,0:T(8,128)(2,1)S(1)} %slice.63.refs_0_), channel_id=1, source_target_pairs={{0,8},{8,16},{16,24},{24,28},{28,20},{20,12},{12,4},{4,0},{1,9},{9... | collective-permute-start | bytes 4718600 | tf_op jit(solution)/shard_map/ppermute | solution.py:408
  105.2 42.7 %collective-permute-start.11 = (bf16[3,512,512]{2,1,0:T(8,128)(2,1)S(1)}, bf16[3,512,512]{2,1,0:T(8,128)(2,1)}, u32[]{:S(2)}, u32[]{:S(2)}) collective-permute-start(bf16[3,512,512]{2,1,0:T(8,128)(2,1)S(1)} %slice.63.refs_0_), channel_id=1, source_target_pairs={{8,0},{16,8},{24,16},{28,24},{20,28},{12,20},{4,12},{0,4},{9,1},{1... | collective-permute-start | bytes 4718600 | tf_op jit(solution)/shard_map/ppermute | solution.py:409
  149.3 37.2 %collective-permute-start.23 = (bf16[3,512,512]{2,1,0:T(8,128)(2,1)}, bf16[3,512,512]{2,1,0:T(8,128)(2,1)S(1)}, u32[]{:S(2)}, u32[]{:S(2)}) collective-permute-start(bf16[3,512,512]{2,1,0:T(8,128)(2,1)} %collective-permute-done.10.refs_1_), channel_id=1, source_target_pairs={{0,8},{8,16},{16,24},{24,28},{28,20},{20,12},{12,4},{4,0},{1,9},{9... | collective-permute-start | bytes 4718600 | tf_op jit(solution)/shard_map/ppermute | solution.py:408
  150.8 36.7 %collective-permute-start.25 = (bf16[3,512,512]{2,1,0:T(8,128)(2,1)}, bf16[3,512,512]{2,1,0:T(8,128)(2,1)S(1)}, u32[]{:S(2)}, u32[]{:S(2)}) collective-permute-start(bf16[3,512,512]{2,1,0:T(8,128)(2,1)} %collective-permute-done.11.refs_5_), channel_id=1, source_target_pairs={{8,0},{16,8},{24,16},{28,24},{20,28},{12,20},{4,12},{0,4},{9,1},{1... | collective-permute-start | bytes 4718600 | tf_op jit(solution)/shard_map/ppermute | solution.py:409
  186.3 47.8 %collective-permute-start.31 = (bf16[1040,1024]{1,0:T(8,128)(2,1)S(1)}, bf16[1040,1024]{1,0:T(8,128)(2,1)}, u32[]{:S(2)}, u32[]{:S(2)}) collective-permute-start(bf16[1040,1024]{1,0:T(8,128)(2,1)S(1)} %constant_dynamic-update-slice_fusion.4.refs_0_), channel_id=1, source_target_pairs={{0,2},{1,3},{2,0},{3,1},{4,6},{5,7},{6,4},{7,5},{8,10},{9,11},{10,... | collective-permute-start | bytes 6389768 | tf_op jit(solution)/shard_map/ppermute | solution.py:433
  187.6 46.5 %collective-permute-start.27 = (bf16[3,512,256]{2,1,0:T(8,128)(2,1)S(1)}, bf16[3,512,256]{2,1,0:T(8,128)(2,1)S(1)}, u32[]{:S(2)}, u32[]{:S(2)}) collective-permute-start(bf16[3,512,256]{2,1,0:T(8,128)(2,1)S(1)} %get-tuple-element.74.refs_0_), channel_id=1, source_target_pairs={{0,8},{8,16},{16,24},{24,28},{28,20},{20,12},{12,4},{4,0},{1,9},{9... | collective-permute-start | bytes 2359304 | tf_op jit(solution)/shard_map/ppermute | solution.py:408
  188.7 54.0 %collective-permute-start.24 = (bf16[3,512,512]{2,1,0:T(8,128)(2,1)S(1)}, bf16[3,512,512]{2,1,0:T(8,128)(2,1)S(1)}, u32[]{:S(2)}, u32[]{:S(2)}) collective-permute-start(bf16[3,512,512]{2,1,0:T(8,128)(2,1)S(1)} %collective-permute-done.23.refs_2_), channel_id=1, source_target_pairs={{0,8},{8,16},{16,24},{24,28},{28,20},{20,12},{12,4},{4,0},{1,9},{9... | collective-permute-start | bytes 4718600 | tf_op jit(solution)/shard_map/ppermute | solution.py:408
  190.2 56.3 %collective-permute-start.26 = (bf16[3,512,512]{2,1,0:T(8,128)(2,1)S(1)}, bf16[3,512,512]{2,1,0:T(8,128)(2,1)S(1)}, u32[]{:S(2)}, u32[]{:S(2)}) collective-permute-start(bf16[3,512,512]{2,1,0:T(8,128)(2,1)S(1)} %collective-permute-done.25.refs_6_), channel_id=1, source_target_pairs={{8,0},{16,8},{24,16},{28,24},{20,28},{12,20},{4,12},{0,4},{9,1},{1... | collective-permute-start | bytes 4718600 | tf_op jit(solution)/shard_map/ppermute | solution.py:409
  191.9 50.4 %collective-permute-start.28 = (bf16[3,512,256]{2,1,0:T(8,128)(2,1)S(1)}, bf16[3,512,256]{2,1,0:T(8,128)(2,1)}, u32[]{:S(2)}, u32[]{:S(2)}) collective-permute-start(bf16[3,512,256]{2,1,0:T(8,128)(2,1)S(1)} %get-tuple-element.74.refs_0_), channel_id=1, source_target_pairs={{8,0},{16,8},{24,16},{28,24},{20,28},{12,20},{4,12},{0,4},{9,1},{1... | collective-permute-start | bytes 2359304 | tf_op jit(solution)/shard_map/ppermute | solution.py:409
  234.1 43.5 %collective-permute-start.30 = (bf16[1040,1024]{1,0:T(8,128)(2,1)S(1)}, bf16[1040,1024]{1,0:T(8,128)(2,1)}, u32[]{:S(2)}, u32[]{:S(2)}) collective-permute-start(bf16[1040,1024]{1,0:T(8,128)(2,1)S(1)} %constant_dynamic-update-slice_fusion.4.refs_0_), channel_id=1, source_target_pairs={{0,1},{1,0},{2,3},{3,2},{4,5},{5,4},{6,7},{7,6},{8,9},{9,8},{10,11... | collective-permute-start | bytes 6389768 | tf_op jit(solution)/shard_map/ppermute | solution.py:433
  234.1 43.5 %collective-permute-start.32 = (bf16[1040,1024]{1,0:T(8,128)(2,1)}, bf16[1040,1024]{1,0:T(8,128)(2,1)}, u32[]{:S(2)}, u32[]{:S(2)}) collective-permute-start(bf16[1040,1024]{1,0:T(8,128)(2,1)} %collective-permute-done.31.refs_2_), channel_id=1, source_target_pairs={{0,1},{1,0},{2,3},{3,2},{4,5},{5,4},{6,7},{7,6},{8,9},{9,8},{10,11... | collective-permute-start | bytes 6389768 | tf_op jit(solution)/shard_map/ppermute | solution.py:433
  246.5 30.2 %collective-permute-start.33 = (bf16[3,256,512]{2,1,0:T(8,128)(2,1)}, bf16[3,256,512]{2,1,0:T(8,128)(2,1)}, u32[]{:S(2)}, u32[]{:S(2)}) collective-permute-start(bf16[3,256,512]{2,1,0:T(8,128)(2,1)} %slice.67), channel_id=1, source_target_pairs={{0,8},{8,16},{16,24},{24,28},{28,20},{20,12},{12,4},{4,0},{1,9},{9... | collective-permute-start | bytes 2359304 | tf_op jit(solution)/shard_map/ppermute | solution.py:408
  290.9 46.3 %collective-permute-start.41 = (bf16[3,512,256]{2,1,0:T(8,128)(2,1)S(1)}, bf16[3,512,256]{2,1,0:T(8,128)(2,1)S(1)}, u32[]{:S(2)}, u32[]{:S(2)}) collective-permute-start(bf16[3,512,256]{2,1,0:T(8,128)(2,1)S(1)} %get-tuple-element.89.refs_0_), channel_id=1, source_target_pairs={{0,8},{8,16},{16,24},{24,28},{28,20},{20,12},{12,4},{4,0},{1,9},{9... | collective-permute-start | bytes 2359304 | tf_op jit(solution)/shard_map/ppermute | solution.py:408
  291.1 46.1 %collective-permute-start.42 = (bf16[3,512,256]{2,1,0:T(8,128)(2,1)S(1)}, bf16[3,512,256]{2,1,0:T(8,128)(2,1)S(1)}, u32[]{:S(2)}, u32[]{:S(2)}) collective-permute-start(bf16[3,512,256]{2,1,0:T(8,128)(2,1)S(1)} %get-tuple-element.89.refs_0_), channel_id=1, source_target_pairs={{8,0},{16,8},{24,16},{28,24},{20,28},{12,20},{4,12},{0,4},{9,1},{1... | collective-permute-start | bytes 2359304 | tf_op jit(solution)/shard_map/ppermute | solution.py:409
  293.0 46.3 %collective-permute-start.37 = (bf16[3,512,256]{2,1,0:T(8,128)(2,1)S(1)}, bf16[3,512,256]{2,1,0:T(8,128)(2,1)S(1)}, u32[]{:S(2)}, u32[]{:S(2)}) collective-permute-start(bf16[3,512,256]{2,1,0:T(8,128)(2,1)S(1)} %copy-done.14), channel_id=1, source_target_pairs={{0,8},{8,16},{16,24},{24,28},{28,20},{20,12},{12,4},{4,0},{1,9},{9... | collective-permute-start | bytes 2359304 | tf_op jit(solution)/shard_map/ppermute | solution.py:408
  293.2 46.2 %collective-permute-start.38 = (bf16[3,512,256]{2,1,0:T(8,128)(2,1)}, bf16[3,512,256]{2,1,0:T(8,128)(2,1)S(1)}, u32[]{:S(2)}, u32[]{:S(2)}) collective-permute-start(bf16[3,512,256]{2,1,0:T(8,128)(2,1)} %collective-permute-done.36.refs_6_), channel_id=1, source_target_pairs={{8,0},{16,8},{24,16},{28,24},{20,28},{12,20},{4,12},{0,4},{9,1},{1... | collective-permute-start | bytes 2359304 | tf_op jit(solution)/shard_map/ppermute | solution.py:409
  339.4 26.8 %collective-permute-start.39 = (bf16[3,256,256]{2,1,0:T(8,128)(2,1)S(1)}, bf16[3,256,256]{2,1,0:T(8,128)(2,1)S(1)}, u32[]{:S(2)}, u32[]{:S(2)}) collective-permute-start(bf16[3,256,256]{2,1,0:T(8,128)(2,1)S(1)} %slice.69), channel_id=1, source_target_pairs={{0,8},{8,16},{16,24},{24,28},{28,20},{20,12},{12,4},{4,0},{1,9},{9... | collective-permute-start | bytes 1179656 | tf_op jit(solution)/shard_map/ppermute | solution.py:408
  339.6 26.7 %collective-permute-start.40 = (bf16[3,256,256]{2,1,0:T(8,128)(2,1)S(1)}, bf16[3,256,256]{2,1,0:T(8,128)(2,1)S(1)}, u32[]{:S(2)}, u32[]{:S(2)}) collective-permute-start(bf16[3,256,256]{2,1,0:T(8,128)(2,1)S(1)} %slice.70), channel_id=1, source_target_pairs={{8,0},{16,8},{24,16},{28,24},{20,28},{12,20},{4,12},{0,4},{9,1},{1... | collective-permute-start | bytes 1179656 | tf_op jit(solution)/shard_map/ppermute | solution.py:409
  357.7 26.8 %collective-permute-start.44 = (bf16[3,512,256]{2,1,0:T(8,128)(2,1)S(1)}, bf16[3,512,256]{2,1,0:T(8,128)(2,1)S(1)}, u32[]{:S(2)}, u32[]{:S(2)}) collective-permute-start(bf16[3,512,256]{2,1,0:T(8,128)(2,1)S(1)} %collective-permute-done.43.refs_2_), channel_id=1, source_target_pairs={{0,8},{8,16},{16,24},{24,28},{28,20},{20,12},{12,4},{4,0},{1,9},{9... | collective-permute-start | bytes 2359304 | tf_op jit(solution)/shard_map/ppermute | solution.py:408
  357.9 26.7 %collective-permute-start.46 = (bf16[3,512,256]{2,1,0:T(8,128)(2,1)S(1)}, bf16[3,512,256]{2,1,0:T(8,128)(2,1)S(1)}, u32[]{:S(2)}, u32[]{:S(2)}) collective-permute-start(bf16[3,512,256]{2,1,0:T(8,128)(2,1)S(1)} %collective-permute-done.45.refs_6_), channel_id=1, source_target_pairs={{8,0},{16,8},{24,16},{28,24},{20,28},{12,20},{4,12},{0,4},{9,1},{1... | collective-permute-start | bytes 2359304 | tf_op jit(solution)/shard_map/ppermute | solution.py:409
  (90 other events, 1473.4 us)

commit v3 on v2

--- a/solution.py
+++ b/solution.py
@@ -543,7 +543,6 @@
     shared = tp_pieces(extended, n_tp, drive(steps + 1))
     turn = steps + 2
     normed = norm_rows(after(gain, drive(turn)), shared)
-    hold(turn, normed)
 
     lr_taps = lr_short.transpose(1, 0, 2)
     found = []
@@ -554,11 +553,11 @@
         taps = lr_taps
         for part in range(width // CHUNK):
             if part > 0:
-                taps = after(lr_taps, drive(turn + 1))
+                taps = after(lr_taps, drive(turn + 2))
             found.append(
                 lr_local(cols, normed, taps, lr_rate, lr_residue, rings[i + 1].blocks(), first, part)
             )
-            hold(turn + 1, found[-1][3])
+            hold(turn + 1 + part, found[-1][3])
         first += width
     odd, other, fars = earlier_states(
         jnp.concatenate([f[3] for f in found], axis=1), lr_rate, rows

time: 444 us -> 438 us (0.986)
  waiting for transfers between devices: 161 us -> 156 us
    ppermute x16, waiting for transfers between devices: 17.6 us -> 8.74 us  [step(): self.behind.append(lax.ppermute(b, 'seq', self.left))]
    ppermute x16, starting transfers between devices: 16.4 us -> 24.3 us  [step(): self.ahead.append(lax.ppermute(a, 'seq', self.right))]
    ppermute x16, starting transfers between devices: 17.5 us -> 10.4 us  [step(): self.behind.append(lax.ppermute(b, 'seq', self.left))]
    unnamed x126 -> x134, local copies, waits for them, and re-layouts: 27.4 us -> 25.8 us
  transfers between devices with their start and end apart: 53 -> 53, of which waited for: 24 -> 24; matrix products, arithmetic and copies ran while one was open for 2% -> 3% of each run, Pallas kernels for 33% -> 36%
where the time goes in v3:
time: 438 us; the launch traced here: 437 us
  Pallas kernels  184 us (42%)
  waiting for transfers between devices  156 us (36%)
  starting transfers between devices  55.2 us (13%)
  local copies, waits for them, and re-layouts  37.7 us (9%)
    pallas_call x4, Pallas kernels, lr_local(): pl.pallas_call(functools.partial(lr_kernel, len(blocks), part), grid=(1,)...  75.9 us
    pallas_call x4, Pallas kernels, mr_operator(): pl.pallas_call(mr_kernel, grid=(count // LANES,), out_shape=jax.ShapeDtyp...  72.1 us
    ppermute x16, waiting for transfers between devices, step(): self.ahead.append(lax.ppermute(a, 'seq', self.right))  65.1 us
    ppermute x15, waiting for transfers between devices, swap_tp(): return lax.ppermute(value, 'tp', [(i, i ^ mask) for i in range(count)])  54.5 us
    unnamed x134, local copies, waits for them, and re-layouts  25.8 us
    ppermute x5, waiting for transfers between devices, from_behind(): lax.ppermute(value, 'seq', [(i, i + steps) for i in range(count - steps)])  24.5 us
    ppermute x16, starting transfers between devices, step(): self.ahead.append(lax.ppermute(a, 'seq', self.right))  24.3 us
    pallas_call x1, Pallas kernels, stream_rows(): pl.pallas_call(functools.partial(stream_kernel, len(pieces), len(blocks))...  17.2 us
  transfers between devices with their start and end apart: 53, of which 24 were waited for; matrix products, arithmetic and copies ran while one was open for 3% of the time, Pallas kernels for 36%

profile of v3, /device:TPU:0, one launch (start us, length us, event | category | flops | bytes accessed | tf_op | source)
XLA Modules:
  0.0 437.0 jit_solution(16352910907418253295)
XLA Ops:
  2.0 4.9 %collective-permute-start = (bf16[3,144,1024]{2,1,0:T(8,128)(2,1)S(1)}, bf16[3,144,1024]{2,1,0:T(8,128)(2,1)S(1)}, u32[]{:S(2)}, u32[]{:S(2)}) collective-permute-start(bf16[3,144,1024]{2,1,0:T(8,128)(2,1)S(1)} %slice.60), channel_id=1, source_target_pairs={{0,4},{4,8},{8,12},{12,16},{16,20},{20,24},{24,28},{1,5},{5,9},{9,... | collective-permute-start | bytes 2654216 | tf_op jit(solution)/shard_map/ppermute | solution.py:446
  8.4 17.3 %collective-permute-done.halo_ref = bf16[3,144,1024]{2,1,0:T(8,128)(2,1)S(1)} collective-permute-done((bf16[3,144,1024]{2,1,0:T(8,128)(2,1)S(1)}, bf16[3,144,1024]{2,1,0:T(8,128)(2,1)S(1)}, u32[]{:S(2)}, u32[]{:S(2)}) %collective-permute-start) | collective-permute-done | bytes 884768 | tf_op jit(solution)/shard_map/ppermute | solution.py:446
  25.7 3.5 collective-permute-start.1
  32.0 17.9 %mr_operator.4.refs_0_ = bf16[1024,256]{1,0:T(8,128)(2,1)S(1)} custom-call(bf16[3,144,1024]{2,1,0:T(8,128)(2,1)S(1)} %collective-permute-done.halo_ref, bf16[3,1024,1024]{2,1,0:T(8,128)(2,1)S(1)} %bitcast.13, f32[3,7,1024]{2,1,0:T(8,128)S(1)} %bitcast.18, bf16[128,1024]{1,0:T(8,128)(2,1)S(1)} %copy-done.31), custom_call_target="tpu_custom_call" | custom-call | flops 20499660800 | tf_op jit(solution)/shard_map/mr_operator/pallas_call | solution.py:109
  55.0 17.9 %mr_operator.5.refs_1_ = bf16[1024,256]{1,0:T(8,128)(2,1)S(1)} custom-call(bf16[3,144,1024]{2,1,0:T(8,128)(2,1)S(1)} %collective-permute-done.halo_ref, bf16[3,1024,1024]{2,1,0:T(8,128)(2,1)S(1)} %bitcast.14, f32[3,7,1024]{2,1,0:T(8,128)S(1)} %bitcast.19, bf16[128,1024]{1,0:T(8,128)(2,1)S(1)} %copy-done.31), custom_call_target="tpu_custom_call" | custom-call | flops 20499660800 | tf_op jit(solution)/shard_map/mr_operator/pallas_call | solution.py:109
  79.1 17.9 %mr_operator.6.refs_2_ = bf16[1024,256]{1,0:T(8,128)(2,1)S(1)} custom-call(bf16[3,144,1024]{2,1,0:T(8,128)(2,1)S(1)} %collective-permute-done.halo_ref, bf16[3,1024,1024]{2,1,0:T(8,128)(2,1)S(1)} %bitcast.15, f32[3,7,1024]{2,1,0:T(8,128)S(1)} %bitcast.20, bf16[128,1024]{1,0:T(8,128)(2,1)S(1)} %copy-done.31), custom_call_target="tpu_custom_call" | custom-call | flops 20499660800 | tf_op jit(solution)/shard_map/mr_operator/pallas_call | solution.py:109
  105.7 18.5 %mr_operator.7.refs_3_ = bf16[1024,256]{1,0:T(8,128)(2,1)} custom-call(bf16[3,144,1024]{2,1,0:T(8,128)(2,1)S(1)} %collective-permute-done.halo_ref, bf16[3,1024,1024]{2,1,0:T(8,128)(2,1)S(1)} %bitcast.16, f32[3,7,1024]{2,1,0:T(8,128)S(1)} %bitcast.21, bf16[128,1024]{1,0:T(8,128)(2,1)S(1)} %copy-done.31), custom_call_target="tpu_custom_call" | custom-call | flops 20499660800 | tf_op jit(solution)/shard_map/mr_operator/pallas_call | solution.py:109
  128.8 12.4 %collective-permute-done.19.refs_11_ = bf16[1024,256]{1,0:T(8,128)(2,1)} collective-permute-done((bf16[1024,256]{1,0:T(8,128)(2,1)}, bf16[1024,256]{1,0:T(8,128)(2,1)}, u32[]{:S(2)}, u32[]{:S(2)}) %collective-permute-start.19) | collective-permute-done | bytes 524320 | tf_op jit(solution)/shard_map/ppermute | solution.py:433
  141.2 4.8 %collective-permute-done.10.refs_1_ = bf16[3,512,512]{2,1,0:T(8,128)(2,1)} collective-permute-done((bf16[3,512,512]{2,1,0:T(8,128)(2,1)S(1)}, bf16[3,512,512]{2,1,0:T(8,128)(2,1)}, u32[]{:S(2)}, u32[]{:S(2)}) %collective-permute-start.10) | collective-permute-done | bytes 1572896 | tf_op jit(solution)/shard_map/ppermute | solution.py:408
  157.6 17.2 %stream_rows.1 = bf16[1040,1024]{1,0:T(8,128)(2,1)} custom-call(s32[9]{0:T(128)S(1)} %fusion.cols_ref, bf16[1024,1024]{1,0:T(8,128)(2,1)} %resid_ref.1, bf16[1024,256]{1,0:T(8,128)(2,1)S(1)} %mr_operator.4.refs_0_, bf16[1024,256]{1,0:T(8,128)(2,1)S(1)} %mr_operator.5.refs_1_, bf16[1024,256]{1,0:T(8,128)(2,1)S(1)} %copy-done.24, ...), custom_call_target="tpu_custom_call" | custom-call | flops 19756849152 | tf_op jit(solution)/shard_map/stream_rows/pallas_call | solution.py:173
  181.0 5.3 %collective-permute-done.29 = bf16[16,1024]{1,0:T(8,128)(2,1)S(1)} collective-permute-done((bf16[16,1024]{1,0:T(8,128)(2,1)S(1)}, bf16[16,1024]{1,0:T(8,128)(2,1)S(1)}, u32[]{:S(2)}, u32[]{:S(2)}) %collective-permute-start.29) | collective-permute-done | bytes 32800 | tf_op jit(solution)/shard_map/ppermute | solution.py:446
  192.0 42.0 %collective-permute-done.31.refs_2_ = bf16[1040,1024]{1,0:T(8,128)(2,1)} collective-permute-done((bf16[1040,1024]{1,0:T(8,128)(2,1)S(1)}, bf16[1040,1024]{1,0:T(8,128)(2,1)}, u32[]{:S(2)}, u32[]{:S(2)}) %collective-permute-start.31) | collective-permute-done | bytes 2129952 | tf_op jit(solution)/shard_map/ppermute | solution.py:433
  234.1 5.6 %collective-permute-done.27.refs_1_ = bf16[3,512,256]{2,1,0:T(8,128)(2,1)S(1)} collective-permute-done((bf16[3,512,256]{2,1,0:T(8,128)(2,1)S(1)}, bf16[3,512,256]{2,1,0:T(8,128)(2,1)S(1)}, u32[]{:S(2)}, u32[]{:S(2)}) %collective-permute-start.27) | collective-permute-done | bytes 786464 | tf_op jit(solution)/shard_map/ppermute | solution.py:408
  245.4 15.7 %collective-permute-done.35.refs_2_ = bf16[3,512,256]{2,1,0:T(8,128)(2,1)} collective-permute-done((bf16[3,512,256]{2,1,0:T(8,128)(2,1)S(1)}, bf16[3,512,256]{2,1,0:T(8,128)(2,1)}, u32[]{:S(2)}, u32[]{:S(2)}) %collective-permute-start.35) | collective-permute-done | bytes 786464 | tf_op jit(solution)/shard_map/ppermute | solution.py:408
  263.2 14.7 %collective-permute-done.33.refs_4_ = bf16[3,256,512]{2,1,0:T(8,128)(2,1)S(1)} collective-permute-done((bf16[3,256,512]{2,1,0:T(8,128)(2,1)S(1)}, bf16[3,256,512]{2,1,0:T(8,128)(2,1)S(1)}, u32[]{:S(2)}, u32[]{:S(2)}) %collective-permute-start.33) | collective-permute-done | bytes 786464 | tf_op jit(solution)/shard_map/ppermute | solution.py:408
  281.6 13.3 %collective-permute-done.36.refs_3_ = bf16[3,512,256]{2,1,0:T(8,128)(2,1)} collective-permute-done((bf16[3,512,256]{2,1,0:T(8,128)(2,1)}, bf16[3,512,256]{2,1,0:T(8,128)(2,1)}, u32[]{:S(2)}, u32[]{:S(2)}) %collective-permute-start.36) | collective-permute-done | bytes 786464 | tf_op jit(solution)/shard_map/ppermute | solution.py:408
  298.4 10.4 %norm_rows.1.a_ref = bf16[1040,4096]{1,0:T(8,128)(2,1)S(1)} custom-call(f32[1,4096]{1,0:T(1,128)S(1)} %bitcast.17, bf16[1040,1024]{1,0:T(8,128)(2,1)S(1)} %constant_dynamic-update-slice_fusion.4.refs_0_, bf16[1040,1024]{1,0:T(8,128)(2,1)} %collective-permute-done.30.refs_1_, bf16[1040,1024]{1,0:T(8,128)(2,1)} %collective-permute-done.31.refs_2_, ...), custom_call_target="tpu_custom_call" | custom-call | flops 10777395200 | tf_op jit(solution)/shard_map/norm_rows/pallas_call | solution.py:205
  308.8 3.4 copy-done.47
  312.2 19.8 %lr_local.4 = (f32[128,8,256]{2,1,0:T(8,128)S(1)}, f32[128,8,256]{2,1,0:T(8,128)S(1)}, f32[16,8,256]{2,1,0:T(8,128)S(1)}, f32[16,256]{1,0:T(8,128)S(1)}) custom-call(s32[9]{0:T(128)S(1)} %fusion.cols_ref, bf16[1040,4096]{1,0:T(8,128)(2,1)} %copy-done.47, f32[3,7,1024]{2,1,0:T(8,128)S(1)} %bitcast.22, f32[16,1024]{1,0:T(8,128)S(1)} %copy-done.8, ...), custom_call_target="tpu_custom_call" | custom-call | flops 20991651840 | tf_op jit(solution)/shard_map/lr_local/pallas_call | solution.py:297
  336.6 19.6 %lr_local.5 = (f32[128,8,256]{2,1,0:T(8,128)S(1)}, f32[128,8,256]{2,1,0:T(8,128)S(1)}, f32[16,8,256]{2,1,0:T(8,128)S(1)}, f32[16,256]{1,0:T(8,128)S(1)}) custom-call(s32[9]{0:T(128)S(1)} %fusion.cols_ref, bf16[1040,4096]{1,0:T(8,128)(2,1)} %copy-done.47, f32[3,7,1024]{2,1,0:T(8,128)S(1)} %bitcast.23, f32[16,1024]{1,0:T(8,128)S(1)} %copy-done.8, ...), custom_call_target="tpu_custom_call" | custom-call | flops 20991651840 | tf_op jit(solution)/shard_map/lr_local/pallas_call | solution.py:297
  360.8 18.7 %lr_local.6 = (f32[128,8,256]{2,1,0:T(8,128)S(1)}, f32[128,8,256]{2,1,0:T(8,128)S(1)}, f32[16,8,256]{2,1,0:T(8,128)S(1)}, f32[16,256]{1,0:T(8,128)S(1)}) custom-call(s32[9]{0:T(128)S(1)} %fusion.cols_ref, bf16[1040,4096]{1,0:T(8,128)(2,1)} %copy-done.47, f32[3,7,1024]{2,1,0:T(8,128)S(1)} %bitcast.24, f32[16,1024]{1,0:T(8,128)S(1)} %copy-done.8, ...), custom_call_target="tpu_custom_call" | custom-call | flops 20991651840 | tf_op jit(solution)/shard_map/lr_local/pallas_call | solution.py:297
  383.6 5.7 %collective-permute-done.47.refs_4_ = bf16[3,256,256]{2,1,0:T(8,128)(2,1)S(1)} collective-permute-done((bf16[3,256,256]{2,1,0:T(8,128)(2,1)S(1)}, bf16[3,256,256]{2,1,0:T(8,128)(2,1)S(1)}, u32[]{:S(2)}, u32[]{:S(2)}) %collective-permute-start.47) | collective-permute-done | bytes 393248 | tf_op jit(solution)/shard_map/ppermute | solution.py:408
  390.5 17.9 %lr_local.7 = (f32[128,8,256]{2,1,0:T(8,128)S(1)}, f32[128,8,256]{2,1,0:T(8,128)S(1)}, f32[16,8,256]{2,1,0:T(8,128)S(1)}, f32[16,256]{1,0:T(8,128)S(1)}) custom-call(s32[9]{0:T(128)S(1)} %fusion.cols_ref, bf16[1040,4096]{1,0:T(8,128)(2,1)} %copy-done.47, f32[3,7,1024]{2,1,0:T(8,128)S(1)} %bitcast.25, f32[16,1024]{1,0:T(8,128)S(1)} %copy-done.8, ...), custom_call_target="tpu_custom_call" | custom-call | flops 20991651840 | tf_op jit(solution)/shard_map/lr_local/pallas_call | solution.py:297
  411.8 3.5 collective-permute-done.49.refs_0_
  (257 shorter events, 107.9 us)
Async XLA Ops:
  25.7 25.7 %collective-permute-start.1 = (bf16[512,1024]{1,0:T(8,128)(2,1)S(1)}, bf16[512,1024]{1,0:T(8,128)(2,1)S(1)}, u32[]{:S(2)}, u32[]{:S(2)}) collective-permute-start(bf16[512,1024]{1,0:T(8,128)(2,1)S(1)} %copy-done.58), channel_id=1, source_target_pairs={{0,8},{8,16},{16,24},{24,28},{28,20},{20,12},{12,4},{4,0},{1,9},{9... | collective-permute-start | bytes 3145736 | tf_op jit(solution)/shard_map/ppermute | solution.py:408
  29.2 23.7 %collective-permute-start.2 = (bf16[512,1024]{1,0:T(8,128)(2,1)S(1)}, bf16[512,1024]{1,0:T(8,128)(2,1)S(1)}, u32[]{:S(2)}, u32[]{:S(2)}) collective-permute-start(bf16[512,1024]{1,0:T(8,128)(2,1)S(1)} %copy-done.58), channel_id=1, source_target_pairs={{8,0},{16,8},{24,16},{28,24},{20,28},{12,20},{4,12},{0,4},{9,1},{1... | collective-permute-start | bytes 3145736 | tf_op jit(solution)/shard_map/ppermute | solution.py:409
  49.9 24.6 %collective-permute-start.7 = (bf16[1024,256]{1,0:T(8,128)(2,1)S(1)}, bf16[1024,256]{1,0:T(8,128)(2,1)S(1)}, u32[]{:S(2)}, u32[]{:S(2)}) collective-permute-start(bf16[1024,256]{1,0:T(8,128)(2,1)S(1)} %mr_operator.4.refs_0_), channel_id=1, source_target_pairs={{0,2},{1,3},{2,0},{3,1},{4,6},{5,7},{6,4},{7,5},{8,10},{9,11},{10,... | collective-permute-start | bytes 1572872 | tf_op jit(solution)/shard_map/ppermute | solution.py:433
  72.9 30.7 %collective-permute-start.12 = (bf16[1024,256]{1,0:T(8,128)(2,1)S(1)}, bf16[1024,256]{1,0:T(8,128)(2,1)S(1)}, u32[]{:S(2)}, u32[]{:S(2)}) collective-permute-start(bf16[1024,256]{1,0:T(8,128)(2,1)S(1)} %mr_operator.5.refs_1_), channel_id=1, source_target_pairs={{0,2},{1,3},{2,0},{3,1},{4,6},{5,7},{6,4},{7,5},{8,10},{9,11},{10,... | collective-permute-start | bytes 1572872 | tf_op jit(solution)/shard_map/ppermute | solution.py:433
  74.5 30.7 %collective-permute-start.13 = (bf16[1024,256]{1,0:T(8,128)(2,1)S(1)}, bf16[1024,256]{1,0:T(8,128)(2,1)S(1)}, u32[]{:S(2)}, u32[]{:S(2)}) collective-permute-start(bf16[1024,256]{1,0:T(8,128)(2,1)S(1)} %collective-permute-done.7.refs_8_), channel_id=1, source_target_pairs={{0,1},{1,0},{2,3},{3,2},{4,5},{5,4},{6,7},{7,6},{8,9},{9,8},{10,11... | collective-permute-start | bytes 1572872 | tf_op jit(solution)/shard_map/ppermute | solution.py:433
  97.0 29.3 %collective-permute-start.18 = (bf16[1024,256]{1,0:T(8,128)(2,1)S(1)}, bf16[1024,256]{1,0:T(8,128)(2,1)S(1)}, u32[]{:S(2)}, u32[]{:S(2)}) collective-permute-start(bf16[1024,256]{1,0:T(8,128)(2,1)S(1)} %mr_operator.6.refs_2_), channel_id=1, source_target_pairs={{0,2},{1,3},{2,0},{3,1},{4,6},{5,7},{6,4},{7,5},{8,10},{9,11},{10,... | collective-permute-start | bytes 1572872 | tf_op jit(solution)/shard_map/ppermute | solution.py:433
  103.6 42.4 %collective-permute-start.10 = (bf16[3,512,512]{2,1,0:T(8,128)(2,1)S(1)}, bf16[3,512,512]{2,1,0:T(8,128)(2,1)}, u32[]{:S(2)}, u32[]{:S(2)}) collective-permute-start(bf16[3,512,512]{2,1,0:T(8,128)(2,1)S(1)} %slice.63.refs_0_), channel_id=1, source_target_pairs={{0,8},{8,16},{16,24},{24,28},{28,20},{20,12},{12,4},{4,0},{1,9},{9... | collective-permute-start | bytes 4718600 | tf_op jit(solution)/shard_map/ppermute | solution.py:408
  105.2 42.7 %collective-permute-start.11 = (bf16[3,512,512]{2,1,0:T(8,128)(2,1)S(1)}, bf16[3,512,512]{2,1,0:T(8,128)(2,1)}, u32[]{:S(2)}, u32[]{:S(2)}) collective-permute-start(bf16[3,512,512]{2,1,0:T(8,128)(2,1)S(1)} %slice.63.refs_0_), channel_id=1, source_target_pairs={{8,0},{16,8},{24,16},{28,24},{20,28},{12,20},{4,12},{0,4},{9,1},{1... | collective-permute-start | bytes 4718600 | tf_op jit(solution)/shard_map/ppermute | solution.py:409
  149.3 37.1 %collective-permute-start.23 = (bf16[3,512,512]{2,1,0:T(8,128)(2,1)}, bf16[3,512,512]{2,1,0:T(8,128)(2,1)S(1)}, u32[]{:S(2)}, u32[]{:S(2)}) collective-permute-start(bf16[3,512,512]{2,1,0:T(8,128)(2,1)} %collective-permute-done.10.refs_1_), channel_id=1, source_target_pairs={{0,8},{8,16},{16,24},{24,28},{28,20},{20,12},{12,4},{4,0},{1,9},{9... | collective-permute-start | bytes 4718600 | tf_op jit(solution)/shard_map/ppermute | solution.py:408
  150.8 37.7 %collective-permute-start.25 = (bf16[3,512,512]{2,1,0:T(8,128)(2,1)}, bf16[3,512,512]{2,1,0:T(8,128)(2,1)S(1)}, u32[]{:S(2)}, u32[]{:S(2)}) collective-permute-start(bf16[3,512,512]{2,1,0:T(8,128)(2,1)} %collective-permute-done.11.refs_5_), channel_id=1, source_target_pairs={{8,0},{16,8},{24,16},{28,24},{20,28},{12,20},{4,12},{0,4},{9,1},{1... | collective-permute-start | bytes 4718600 | tf_op jit(solution)/shard_map/ppermute | solution.py:409
  186.3 47.8 %collective-permute-start.31 = (bf16[1040,1024]{1,0:T(8,128)(2,1)S(1)}, bf16[1040,1024]{1,0:T(8,128)(2,1)}, u32[]{:S(2)}, u32[]{:S(2)}) collective-permute-start(bf16[1040,1024]{1,0:T(8,128)(2,1)S(1)} %constant_dynamic-update-slice_fusion.4.refs_0_), channel_id=1, source_target_pairs={{0,2},{1,3},{2,0},{3,1},{4,6},{5,7},{6,4},{7,5},{8,10},{9,11},{10,... | collective-permute-start | bytes 6389768 | tf_op jit(solution)/shard_map/ppermute | solution.py:433
  186.3 54.8 %collective-permute-start.24 = (bf16[3,512,512]{2,1,0:T(8,128)(2,1)S(1)}, bf16[3,512,512]{2,1,0:T(8,128)(2,1)S(1)}, u32[]{:S(2)}, u32[]{:S(2)}) collective-permute-start(bf16[3,512,512]{2,1,0:T(8,128)(2,1)S(1)} %collective-permute-done.23.refs_2_), channel_id=1, source_target_pairs={{0,8},{8,16},{16,24},{24,28},{28,20},{20,12},{12,4},{4,0},{1,9},{9... | collective-permute-start | bytes 4718600 | tf_op jit(solution)/shard_map/ppermute | solution.py:408
  188.6 55.3 %collective-permute-start.26 = (bf16[3,512,512]{2,1,0:T(8,128)(2,1)S(1)}, bf16[3,512,512]{2,1,0:T(8,128)(2,1)S(1)}, u32[]{:S(2)}, u32[]{:S(2)}) collective-permute-start(bf16[3,512,512]{2,1,0:T(8,128)(2,1)S(1)} %collective-permute-done.25.refs_6_), channel_id=1, source_target_pairs={{8,0},{16,8},{24,16},{28,24},{20,28},{12,20},{4,12},{0,4},{9,1},{1... | collective-permute-start | bytes 4718600 | tf_op jit(solution)/shard_map/ppermute | solution.py:409
  189.1 50.6 %collective-permute-start.27 = (bf16[3,512,256]{2,1,0:T(8,128)(2,1)S(1)}, bf16[3,512,256]{2,1,0:T(8,128)(2,1)S(1)}, u32[]{:S(2)}, u32[]{:S(2)}) collective-permute-start(bf16[3,512,256]{2,1,0:T(8,128)(2,1)S(1)} %get-tuple-element.74.refs_0_), channel_id=1, source_target_pairs={{0,8},{8,16},{16,24},{24,28},{28,20},{20,12},{12,4},{4,0},{1,9},{9... | collective-permute-start | bytes 2359304 | tf_op jit(solution)/shard_map/ppermute | solution.py:408
  190.8 49.8 %collective-permute-start.28 = (bf16[3,512,256]{2,1,0:T(8,128)(2,1)S(1)}, bf16[3,512,256]{2,1,0:T(8,128)(2,1)S(1)}, u32[]{:S(2)}, u32[]{:S(2)}) collective-permute-start(bf16[3,512,256]{2,1,0:T(8,128)(2,1)S(1)} %get-tuple-element.74.refs_0_), channel_id=1, source_target_pairs={{8,0},{16,8},{24,16},{28,24},{20,28},{12,20},{4,12},{0,4},{9,1},{1... | collective-permute-start | bytes 2359304 | tf_op jit(solution)/shard_map/ppermute | solution.py:409
  234.0 64.3 %collective-permute-start.30 = (bf16[1040,1024]{1,0:T(8,128)(2,1)S(1)}, bf16[1040,1024]{1,0:T(8,128)(2,1)}, u32[]{:S(2)}, u32[]{:S(2)}) collective-permute-start(bf16[1040,1024]{1,0:T(8,128)(2,1)S(1)} %constant_dynamic-update-slice_fusion.4.refs_0_), channel_id=1, source_target_pairs={{0,1},{1,0},{2,3},{3,2},{4,5},{5,4},{6,7},{7,6},{8,9},{9,8},{10,11... | collective-permute-start | bytes 6389768 | tf_op jit(solution)/shard_map/ppermute | solution.py:433
  239.7 58.7 %collective-permute-start.32 = (bf16[1040,1024]{1,0:T(8,128)(2,1)}, bf16[1040,1024]{1,0:T(8,128)(2,1)}, u32[]{:S(2)}, u32[]{:S(2)}) collective-permute-start(bf16[1040,1024]{1,0:T(8,128)(2,1)} %collective-permute-done.31.refs_2_), channel_id=1, source_target_pairs={{0,1},{1,0},{2,3},{3,2},{4,5},{5,4},{6,7},{7,6},{8,9},{9,8},{10,11... | collective-permute-start | bytes 6389768 | tf_op jit(solution)/shard_map/ppermute | solution.py:433
  243.8 34.0 %collective-permute-start.33 = (bf16[3,256,512]{2,1,0:T(8,128)(2,1)S(1)}, bf16[3,256,512]{2,1,0:T(8,128)(2,1)S(1)}, u32[]{:S(2)}, u32[]{:S(2)}) collective-permute-start(bf16[3,256,512]{2,1,0:T(8,128)(2,1)S(1)} %slice.67), channel_id=1, source_target_pairs={{0,8},{8,16},{16,24},{24,28},{28,20},{20,12},{12,4},{4,0},{1,9},{9... | collective-permute-start | bytes 2359304 | tf_op jit(solution)/shard_map/ppermute | solution.py:408
  262.0 32.9 %collective-permute-start.36 = (bf16[3,512,256]{2,1,0:T(8,128)(2,1)}, bf16[3,512,256]{2,1,0:T(8,128)(2,1)}, u32[]{:S(2)}, u32[]{:S(2)}) collective-permute-start(bf16[3,512,256]{2,1,0:T(8,128)(2,1)} %collective-permute-done.35.refs_2_), channel_id=1, source_target_pairs={{0,8},{8,16},{16,24},{24,28},{28,20},{20,12},{12,4},{4,0},{1,9},{9... | collective-permute-start | bytes 2359304 | tf_op jit(solution)/shard_map/ppermute | solution.py:408
  280.3 54.3 %collective-permute-start.39 = (bf16[3,512,256]{2,1,0:T(8,128)(2,1)S(1)}, bf16[3,512,256]{2,1,0:T(8,128)(2,1)S(1)}, u32[]{:S(2)}, u32[]{:S(2)}) collective-permute-start(bf16[3,512,256]{2,1,0:T(8,128)(2,1)S(1)} %get-tuple-element.82.refs_0_), channel_id=1, source_target_pairs={{0,8},{8,16},{16,24},{24,28},{28,20},{20,12},{12,4},{4,0},{1,9},{9... | collective-permute-start | bytes 2359304 | tf_op jit(solution)/shard_map/ppermute | solution.py:408
  294.8 39.7 %collective-permute-start.40 = (bf16[3,512,256]{2,1,0:T(8,128)(2,1)S(1)}, bf16[3,512,256]{2,1,0:T(8,128)(2,1)}, u32[]{:S(2)}, u32[]{:S(2)}) collective-permute-start(bf16[3,512,256]{2,1,0:T(8,128)(2,1)S(1)} %get-tuple-element.82.refs_0_), channel_id=1, source_target_pairs={{8,0},{16,8},{24,16},{28,24},{20,28},{12,20},{4,12},{0,4},{9,1},{1... | collective-permute-start | bytes 2359304 | tf_op jit(solution)/shard_map/ppermute | solution.py:409
  332.0 28.8 %collective-permute-start.41 = (bf16[3,256,256]{2,1,0:T(8,128)(2,1)S(1)}, bf16[3,256,256]{2,1,0:T(8,128)(2,1)S(1)}, u32[]{:S(2)}, u32[]{:S(2)}) collective-permute-start(bf16[3,256,256]{2,1,0:T(8,128)(2,1)S(1)} %slice.70), channel_id=1, source_target_pairs={{0,8},{8,16},{16,24},{24,28},{28,20},{20,12},{12,4},{4,0},{1,9},{9... | collective-permute-start | bytes 1179656 | tf_op jit(solution)/shard_map/ppermute | solution.py:408
  333.7 27.1 %collective-permute-start.42 = (bf16[3,256,256]{2,1,0:T(8,128)(2,1)S(1)}, bf16[3,256,256]{2,1,0:T(8,128)(2,1)S(1)}, u32[]{:S(2)}, u32[]{:S(2)}) collective-permute-start(bf16[3,256,256]{2,1,0:T(8,128)(2,1)S(1)} %slice.71), channel_id=1, source_target_pairs={{8,0},{16,8},{24,16},{28,24},{20,28},{12,20},{4,12},{0,4},{9,1},{1... | collective-permute-start | bytes 1179656 | tf_op jit(solution)/shard_map/ppermute | solution.py:409
  334.6 24.0 %collective-permute-start.43 = (bf16[3,512,256]{2,1,0:T(8,128)(2,1)S(1)}, bf16[3,512,256]{2,1,0:T(8,128)(2,1)S(1)}, u32[]{:S(2)}, u32[]{:S(2)}) collective-permute-start(bf16[3,512,256]{2,1,0:T(8,128)(2,1)S(1)} %collective-permute-done.39.refs_1_), channel_id=1, source_target_pairs={{0,8},{8,16},{16,24},{24,28},{28,20},{20,12},{12,4},{4,0},{1,9},{9... | collective-permute-start | bytes 2359304 | tf_op jit(solution)/shard_map/ppermute | solution.py:408
  (94 other events, 1565.9 us)

commit v4 on v3

--- a/solution.py
+++ b/solution.py
@@ -543,6 +543,7 @@
     shared = tp_pieces(extended, n_tp, drive(steps + 1))
     turn = steps + 2
     normed = norm_rows(after(gain, drive(turn)), shared)
+    hold(turn, normed)
 
     lr_taps = lr_short.transpose(1, 0, 2)
     found = []

time: 438 us -> 460 us (1.050)
  waiting for transfers between devices: 156 us -> 179 us
  local copies, waits for them, and re-layouts: 37.7 us -> 31.5 us
    ppermute x16, waiting for transfers between devices: 8.74 us -> 42.2 us  [step(): self.behind.append(lax.ppermute(b, 'seq', self.left))]
    ppermute x15, waiting for transfers between devices: 54.5 us -> 23 us  [swap_tp(): return lax.ppermute(value, 'tp', [(i, i ^ mask) for i in range(count)])]
    ppermute x16, waiting for transfers between devices: 65.1 us -> 91.3 us  [step(): self.ahead.append(lax.ppermute(a, 'seq', self.right))]
    unnamed x134 -> x112, local copies, waits for them, and re-layouts: 25.8 us -> 19.2 us
    ppermute x5, waiting for transfers between devices: 24.5 us -> 19.2 us  [from_behind(): lax.ppermute(value, 'seq', [(i, i + steps) for i in range(count - steps)])]
  transfers between devices with their start and end apart: 53 -> 53, of which waited for: 24 -> 28; matrix products, arithmetic and copies ran while one was open for 3% -> 2% of each run, Pallas kernels for 36% -> 31%
where the time goes in v4:
time: 460 us; the launch traced here: 459 us
  Pallas kernels  185 us (40%)
  waiting for transfers between devices  179 us (39%)
  starting transfers between devices  59.7 us (13%)
  local copies, waits for them, and re-layouts  31.5 us (7%)
    ppermute x16, waiting for transfers between devices, step(): self.ahead.append(lax.ppermute(a, 'seq', self.right))  91.3 us
    pallas_call x4, Pallas kernels, lr_local(): pl.pallas_call(functools.partial(lr_kernel, len(blocks), part), grid=(1,)...  75.8 us
    pallas_call x4, Pallas kernels, mr_operator(): pl.pallas_call(mr_kernel, grid=(count // LANES,), out_shape=jax.ShapeDtyp...  73.3 us
    ppermute x16, waiting for transfers between devices, step(): self.behind.append(lax.ppermute(b, 'seq', self.left))  42.2 us
    ppermute x16, starting transfers between devices, step(): self.ahead.append(lax.ppermute(a, 'seq', self.right))  23.9 us
    ppermute x15, waiting for transfers between devices, swap_tp(): return lax.ppermute(value, 'tp', [(i, i ^ mask) for i in range(count)])  23 us
    unnamed x112, local copies, waits for them, and re-layouts  19.2 us
    ppermute x5, waiting for transfers between devices, from_behind(): lax.ppermute(value, 'seq', [(i, i + steps) for i in range(count - steps)])  19.2 us
  transfers between devices with their start and end apart: 53, of which 28 were waited for; matrix products, arithmetic and copies ran while one was open for 2% of the time, Pallas kernels for 31%

profile of v4, /device:TPU:0, one launch (start us, length us, event | category | flops | bytes accessed | tf_op | source)
XLA Modules:
  0.0 458.6 jit_solution(11108819922465625440)
XLA Ops:
  2.0 4.9 %collective-permute-start = (bf16[3,144,1024]{2,1,0:T(8,128)(2,1)S(1)}, bf16[3,144,1024]{2,1,0:T(8,128)(2,1)S(1)}, u32[]{:S(2)}, u32[]{:S(2)}) collective-permute-start(bf16[3,144,1024]{2,1,0:T(8,128)(2,1)S(1)} %slice.60), channel_id=1, source_target_pairs={{0,4},{4,8},{8,12},{12,16},{16,20},{20,24},{24,28},{1,5},{5,9},{9,... | collective-permute-start | bytes 2654216 | tf_op jit(solution)/shard_map/ppermute | solution.py:446
  8.4 17.3 %collective-permute-done.halo_ref = bf16[3,144,1024]{2,1,0:T(8,128)(2,1)S(1)} collective-permute-done((bf16[3,144,1024]{2,1,0:T(8,128)(2,1)S(1)}, bf16[3,144,1024]{2,1,0:T(8,128)(2,1)S(1)}, u32[]{:S(2)}, u32[]{:S(2)}) %collective-permute-start) | collective-permute-done | bytes 884768 | tf_op jit(solution)/shard_map/ppermute | solution.py:446
  25.7 3.5 collective-permute-start.1
  32.0 18.5 %mr_operator.4.refs_0_ = bf16[1024,256]{1,0:T(8,128)(2,1)} custom-call(bf16[3,144,1024]{2,1,0:T(8,128)(2,1)S(1)} %collective-permute-done.halo_ref, bf16[3,1024,1024]{2,1,0:T(8,128)(2,1)S(1)} %bitcast.13, f32[3,7,1024]{2,1,0:T(8,128)S(1)} %bitcast.18, bf16[128,1024]{1,0:T(8,128)(2,1)S(1)} %copy-done.22), custom_call_target="tpu_custom_call" | custom-call | flops 20499660800 | tf_op jit(solution)/shard_map/mr_operator/pallas_call | solution.py:109
  55.0 18.5 %mr_operator.5.refs_1_ = bf16[1024,256]{1,0:T(8,128)(2,1)} custom-call(bf16[3,144,1024]{2,1,0:T(8,128)(2,1)S(1)} %collective-permute-done.halo_ref, bf16[3,1024,1024]{2,1,0:T(8,128)(2,1)S(1)} %bitcast.14, f32[3,7,1024]{2,1,0:T(8,128)S(1)} %bitcast.19, bf16[128,1024]{1,0:T(8,128)(2,1)S(1)} %copy-done.22), custom_call_target="tpu_custom_call" | custom-call | flops 20499660800 | tf_op jit(solution)/shard_map/mr_operator/pallas_call | solution.py:109
  79.1 17.9 %mr_operator.6.refs_2_ = bf16[1024,256]{1,0:T(8,128)(2,1)S(1)} custom-call(bf16[3,144,1024]{2,1,0:T(8,128)(2,1)S(1)} %collective-permute-done.halo_ref, bf16[3,1024,1024]{2,1,0:T(8,128)(2,1)S(1)} %bitcast.15, f32[3,7,1024]{2,1,0:T(8,128)S(1)} %bitcast.20, bf16[128,1024]{1,0:T(8,128)(2,1)S(1)} %copy-done.22), custom_call_target="tpu_custom_call" | custom-call | flops 20499660800 | tf_op jit(solution)/shard_map/mr_operator/pallas_call | solution.py:109
  106.2 18.5 %mr_operator.7.refs_3_ = bf16[1024,256]{1,0:T(8,128)(2,1)} custom-call(bf16[3,144,1024]{2,1,0:T(8,128)(2,1)S(1)} %collective-permute-done.halo_ref, bf16[3,1024,1024]{2,1,0:T(8,128)(2,1)S(1)} %bitcast.16, f32[3,7,1024]{2,1,0:T(8,128)S(1)} %bitcast.21, bf16[128,1024]{1,0:T(8,128)(2,1)S(1)} %copy-done.22), custom_call_target="tpu_custom_call" | custom-call | flops 20499660800 | tf_op jit(solution)/shard_map/mr_operator/pallas_call | solution.py:109
  129.3 12.4 %collective-permute-done.19.refs_11_ = bf16[1024,256]{1,0:T(8,128)(2,1)} collective-permute-done((bf16[1024,256]{1,0:T(8,128)(2,1)}, bf16[1024,256]{1,0:T(8,128)(2,1)}, u32[]{:S(2)}, u32[]{:S(2)}) %collective-permute-start.19) | collective-permute-done | bytes 524320 | tf_op jit(solution)/shard_map/ppermute | solution.py:433
  141.8 5.2 %collective-permute-done.10.refs_1_ = bf16[3,512,512]{2,1,0:T(8,128)(2,1)S(1)} collective-permute-done((bf16[3,512,512]{2,1,0:T(8,128)(2,1)S(1)}, bf16[3,512,512]{2,1,0:T(8,128)(2,1)S(1)}, u32[]{:S(2)}, u32[]{:S(2)}) %collective-permute-start.10) | collective-permute-done | bytes 1572896 | tf_op jit(solution)/shard_map/ppermute | solution.py:408
  157.8 17.3 %stream_rows.1 = bf16[1040,1024]{1,0:T(8,128)(2,1)} custom-call(s32[9]{0:T(128)S(1)} %fusion.cols_ref, bf16[1024,1024]{1,0:T(8,128)(2,1)} %resid_ref.1, bf16[1024,256]{1,0:T(8,128)(2,1)} %mr_operator.4.refs_0_, bf16[1024,256]{1,0:T(8,128)(2,1)} %mr_operator.5.refs_1_, bf16[1024,256]{1,0:T(8,128)(2,1)S(1)} %copy-done.15, ...), custom_call_target="tpu_custom_call" | custom-call | flops 19756849152 | tf_op jit(solution)/shard_map/stream_rows/pallas_call | solution.py:173
  185.1 34.1 %collective-permute-done.23.refs_2_ = bf16[3,512,512]{2,1,0:T(8,128)(2,1)} collective-permute-done((bf16[3,512,512]{2,1,0:T(8,128)(2,1)S(1)}, bf16[3,512,512]{2,1,0:T(8,128)(2,1)}, u32[]{:S(2)}, u32[]{:S(2)}) %collective-permute-start.23) | collective-permute-done | bytes 1572896 | tf_op jit(solution)/shard_map/ppermute | solution.py:408
  220.1 9.8 %collective-permute-done.31.refs_2_ = bf16[1040,1024]{1,0:T(8,128)(2,1)} collective-permute-done((bf16[1040,1024]{1,0:T(8,128)(2,1)S(1)}, bf16[1040,1024]{1,0:T(8,128)(2,1)}, u32[]{:S(2)}, u32[]{:S(2)}) %collective-permute-start.31) | collective-permute-done | bytes 2129952 | tf_op jit(solution)/shard_map/ppermute | solution.py:433
  234.7 17.4 %collective-permute-done.27.refs_1_ = bf16[3,512,256]{2,1,0:T(8,128)(2,1)} collective-permute-done((bf16[3,512,256]{2,1,0:T(8,128)(2,1)}, bf16[3,512,256]{2,1,0:T(8,128)(2,1)}, u32[]{:S(2)}, u32[]{:S(2)}) %collective-permute-start.27) | collective-permute-done | bytes 786464 | tf_op jit(solution)/shard_map/ppermute | solution.py:408
  254.8 32.3 %collective-permute-done.28.refs_5_ = bf16[3,512,256]{2,1,0:T(8,128)(2,1)} collective-permute-done((bf16[3,512,256]{2,1,0:T(8,128)(2,1)}, bf16[3,512,256]{2,1,0:T(8,128)(2,1)}, u32[]{:S(2)}, u32[]{:S(2)}) %collective-permute-start.28) | collective-permute-done | bytes 786464 | tf_op jit(solution)/shard_map/ppermute | solution.py:409
  293.7 9.8 %norm_rows.1.a_ref = bf16[1040,4096]{1,0:T(8,128)(2,1)S(1)} custom-call(f32[1,4096]{1,0:T(1,128)S(1)} %bitcast.17, bf16[1040,1024]{1,0:T(8,128)(2,1)S(1)} %constant_dynamic-update-slice_fusion.4.refs_0_, bf16[1040,1024]{1,0:T(8,128)(2,1)} %collective-permute-done.30.refs_1_, bf16[1040,1024]{1,0:T(8,128)(2,1)} %collective-permute-done.31.refs_2_, ...), custom_call_target="tpu_custom_call" | custom-call | flops 10777395200 | tf_op jit(solution)/shard_map/norm_rows/pallas_call | solution.py:205
  310.4 14.2 %collective-permute-done.33.refs_4_ = bf16[3,256,512]{2,1,0:T(8,128)(2,1)S(1)} collective-permute-done((bf16[3,256,512]{2,1,0:T(8,128)(2,1)S(1)}, bf16[3,256,512]{2,1,0:T(8,128)(2,1)S(1)}, u32[]{:S(2)}, u32[]{:S(2)}) %collective-permute-start.33) | collective-permute-done | bytes 786464 | tf_op jit(solution)/shard_map/ppermute | solution.py:408
  327.3 19.9 %lr_local.4 = (f32[128,8,256]{2,1,0:T(8,128)S(1)}, f32[128,8,256]{2,1,0:T(8,128)S(1)}, f32[16,8,256]{2,1,0:T(8,128)S(1)}, f32[16,256]{1,0:T(8,128)S(1)}) custom-call(s32[9]{0:T(128)S(1)} %fusion.cols_ref, bf16[1040,4096]{1,0:T(8,128)(2,1)} %copy-done.40, f32[3,7,1024]{2,1,0:T(8,128)S(1)} %bitcast.22, f32[16,1024]{1,0:T(8,128)S(1)} %copy-done.4, ...), custom_call_target="tpu_custom_call" | custom-call | flops 20991651840 | tf_op jit(solution)/shard_map/lr_local/pallas_call | solution.py:297
  347.2 9.2 %collective-permute-done.39.refs_1_ = bf16[3,512,256]{2,1,0:T(8,128)(2,1)S(1)} collective-permute-done((bf16[3,512,256]{2,1,0:T(8,128)(2,1)S(1)}, bf16[3,512,256]{2,1,0:T(8,128)(2,1)S(1)}, u32[]{:S(2)}, u32[]{:S(2)}) %collective-permute-start.39) | collective-permute-done | bytes 786464 | tf_op jit(solution)/shard_map/ppermute | solution.py:408
  360.9 19.9 %lr_local.5 = (f32[128,8,256]{2,1,0:T(8,128)S(1)}, f32[128,8,256]{2,1,0:T(8,128)S(1)}, f32[16,8,256]{2,1,0:T(8,128)S(1)}, f32[16,256]{1,0:T(8,128)S(1)}) custom-call(s32[9]{0:T(128)S(1)} %fusion.cols_ref, bf16[1040,4096]{1,0:T(8,128)(2,1)} %copy-done.40, f32[3,7,1024]{2,1,0:T(8,128)S(1)} %bitcast.23, f32[16,1024]{1,0:T(8,128)S(1)} %copy-done.4, ...), custom_call_target="tpu_custom_call" | custom-call | flops 20991651840 | tf_op jit(solution)/shard_map/lr_local/pallas_call | solution.py:297
  385.9 18.4 %lr_local.6 = (f32[128,8,256]{2,1,0:T(8,128)S(1)}, f32[128,8,256]{2,1,0:T(8,128)S(1)}, f32[16,8,256]{2,1,0:T(8,128)S(1)}, f32[16,256]{1,0:T(8,128)S(1)}) custom-call(s32[9]{0:T(128)S(1)} %fusion.cols_ref, bf16[1040,4096]{1,0:T(8,128)(2,1)} %copy-done.40, f32[3,7,1024]{2,1,0:T(8,128)S(1)} %bitcast.24, f32[16,1024]{1,0:T(8,128)S(1)} %copy-done.4, ...), custom_call_target="tpu_custom_call" | custom-call | flops 20991651840 | tf_op jit(solution)/shard_map/lr_local/pallas_call | solution.py:297
  406.6 5.7 %collective-permute-done.47.refs_4_ = bf16[3,256,256]{2,1,0:T(8,128)(2,1)S(1)} collective-permute-done((bf16[3,256,256]{2,1,0:T(8,128)(2,1)S(1)}, bf16[3,256,256]{2,1,0:T(8,128)(2,1)S(1)}, u32[]{:S(2)}, u32[]{:S(2)}) %collective-permute-start.47) | collective-permute-done | bytes 393248 | tf_op jit(solution)/shard_map/ppermute | solution.py:408
  413.4 17.6 %lr_local.7 = (f32[128,8,256]{2,1,0:T(8,128)S(1)}, f32[128,8,256]{2,1,0:T(8,128)S(1)}, f32[16,8,256]{2,1,0:T(8,128)S(1)}, f32[16,256]{1,0:T(8,128)S(1)}) custom-call(s32[9]{0:T(128)S(1)} %fusion.cols_ref, bf16[1040,4096]{1,0:T(8,128)(2,1)} %copy-done.40, f32[3,7,1024]{2,1,0:T(8,128)S(1)} %bitcast.25, f32[16,1024]{1,0:T(8,128)S(1)} %copy-done.4, ...), custom_call_target="tpu_custom_call" | custom-call | flops 20991651840 | tf_op jit(solution)/shard_map/lr_local/pallas_call | solution.py:297
  433.9 3.4 collective-permute-done.49.refs_0_
  440.7 3.4 collective-permute-start.51
  (235 shorter events, 108.3 us)
Async XLA Ops:
  25.7 26.3 %collective-permute-start.1 = (bf16[512,1024]{1,0:T(8,128)(2,1)S(1)}, bf16[512,1024]{1,0:T(8,128)(2,1)S(1)}, u32[]{:S(2)}, u32[]{:S(2)}) collective-permute-start(bf16[512,1024]{1,0:T(8,128)(2,1)S(1)} %copy-done.47), channel_id=1, source_target_pairs={{0,8},{8,16},{16,24},{24,28},{28,20},{20,12},{12,4},{4,0},{1,9},{9... | collective-permute-start | bytes 3145736 | tf_op jit(solution)/shard_map/ppermute | solution.py:408
  29.2 23.7 %collective-permute-start.2 = (bf16[512,1024]{1,0:T(8,128)(2,1)S(1)}, bf16[512,1024]{1,0:T(8,128)(2,1)S(1)}, u32[]{:S(2)}, u32[]{:S(2)}) collective-permute-start(bf16[512,1024]{1,0:T(8,128)(2,1)S(1)} %copy-done.47), channel_id=1, source_target_pairs={{8,0},{16,8},{24,16},{28,24},{20,28},{12,20},{4,12},{0,4},{9,1},{1... | collective-permute-start | bytes 3145736 | tf_op jit(solution)/shard_map/ppermute | solution.py:409
  50.5 24.5 %collective-permute-start.7 = (bf16[1024,256]{1,0:T(8,128)(2,1)}, bf16[1024,256]{1,0:T(8,128)(2,1)S(1)}, u32[]{:S(2)}, u32[]{:S(2)}) collective-permute-start(bf16[1024,256]{1,0:T(8,128)(2,1)} %mr_operator.4.refs_0_), channel_id=1, source_target_pairs={{0,2},{1,3},{2,0},{3,1},{4,6},{5,7},{6,4},{7,5},{8,10},{9,11},{10,... | collective-permute-start | bytes 1572872 | tf_op jit(solution)/shard_map/ppermute | solution.py:433
  73.5 25.1 %collective-permute-start.12 = (bf16[1024,256]{1,0:T(8,128)(2,1)}, bf16[1024,256]{1,0:T(8,128)(2,1)S(1)}, u32[]{:S(2)}, u32[]{:S(2)}) collective-permute-start(bf16[1024,256]{1,0:T(8,128)(2,1)} %mr_operator.5.refs_1_), channel_id=1, source_target_pairs={{0,2},{1,3},{2,0},{3,1},{4,6},{5,7},{6,4},{7,5},{8,10},{9,11},{10,... | collective-permute-start | bytes 1572872 | tf_op jit(solution)/shard_map/ppermute | solution.py:433
  97.0 29.8 %collective-permute-start.18 = (bf16[1024,256]{1,0:T(8,128)(2,1)S(1)}, bf16[1024,256]{1,0:T(8,128)(2,1)S(1)}, u32[]{:S(2)}, u32[]{:S(2)}) collective-permute-start(bf16[1024,256]{1,0:T(8,128)(2,1)S(1)} %mr_operator.6.refs_2_), channel_id=1, source_target_pairs={{0,2},{1,3},{2,0},{3,1},{4,6},{5,7},{6,4},{7,5},{8,10},{9,11},{10,... | collective-permute-start | bytes 1572872 | tf_op jit(solution)/shard_map/ppermute | solution.py:433
  104.2 42.8 %collective-permute-start.10 = (bf16[3,512,512]{2,1,0:T(8,128)(2,1)S(1)}, bf16[3,512,512]{2,1,0:T(8,128)(2,1)S(1)}, u32[]{:S(2)}, u32[]{:S(2)}) collective-permute-start(bf16[3,512,512]{2,1,0:T(8,128)(2,1)S(1)} %slice.63.refs_0_), channel_id=1, source_target_pairs={{0,8},{8,16},{16,24},{24,28},{28,20},{20,12},{12,4},{4,0},{1,9},{9... | collective-permute-start | bytes 4718600 | tf_op jit(solution)/shard_map/ppermute | solution.py:408
  105.7 42.7 %collective-permute-start.11 = (bf16[3,512,512]{2,1,0:T(8,128)(2,1)S(1)}, bf16[3,512,512]{2,1,0:T(8,128)(2,1)}, u32[]{:S(2)}, u32[]{:S(2)}) collective-permute-start(bf16[3,512,512]{2,1,0:T(8,128)(2,1)S(1)} %slice.63.refs_0_), channel_id=1, source_target_pairs={{8,0},{16,8},{24,16},{28,24},{20,28},{12,20},{4,12},{0,4},{9,1},{1... | collective-permute-start | bytes 4718600 | tf_op jit(solution)/shard_map/ppermute | solution.py:409
  181.6 48.3 %collective-permute-start.31 = (bf16[1040,1024]{1,0:T(8,128)(2,1)S(1)}, bf16[1040,1024]{1,0:T(8,128)(2,1)}, u32[]{:S(2)}, u32[]{:S(2)}) collective-permute-start(bf16[1040,1024]{1,0:T(8,128)(2,1)S(1)} %constant_dynamic-update-slice_fusion.4.refs_0_), channel_id=1, source_target_pairs={{0,2},{1,3},{2,0},{3,1},{4,6},{5,7},{6,4},{7,5},{8,10},{9,11},{10,... | collective-permute-start | bytes 6389768 | tf_op jit(solution)/shard_map/ppermute | solution.py:433
  182.0 37.2 %collective-permute-start.23 = (bf16[3,512,512]{2,1,0:T(8,128)(2,1)S(1)}, bf16[3,512,512]{2,1,0:T(8,128)(2,1)}, u32[]{:S(2)}, u32[]{:S(2)}) collective-permute-start(bf16[3,512,512]{2,1,0:T(8,128)(2,1)S(1)} %copy-done.6), channel_id=1, source_target_pairs={{0,8},{8,16},{16,24},{24,28},{28,20},{20,12},{12,4},{4,0},{1,9},{9... | collective-permute-start | bytes 4718600 | tf_op jit(solution)/shard_map/ppermute | solution.py:408
  185.1 35.0 %collective-permute-start.25 = (bf16[3,512,512]{2,1,0:T(8,128)(2,1)}, bf16[3,512,512]{2,1,0:T(8,128)(2,1)}, u32[]{:S(2)}, u32[]{:S(2)}) collective-permute-start(bf16[3,512,512]{2,1,0:T(8,128)(2,1)} %collective-permute-done.11.refs_5_), channel_id=1, source_target_pairs={{8,0},{16,8},{24,16},{28,24},{20,28},{12,20},{4,12},{0,4},{9,1},{1... | collective-permute-start | bytes 4718600 | tf_op jit(solution)/shard_map/ppermute | solution.py:409
  185.1 107.1 %collective-permute-start.30 = (bf16[1040,1024]{1,0:T(8,128)(2,1)S(1)}, bf16[1040,1024]{1,0:T(8,128)(2,1)}, u32[]{:S(2)}, u32[]{:S(2)}) collective-permute-start(bf16[1040,1024]{1,0:T(8,128)(2,1)S(1)} %constant_dynamic-update-slice_fusion.4.refs_0_), channel_id=1, source_target_pairs={{0,1},{1,0},{2,3},{3,2},{4,5},{5,4},{6,7},{7,6},{8,9},{9,8},{10,11... | collective-permute-start | bytes 6389768 | tf_op jit(solution)/shard_map/ppermute | solution.py:433
  229.9 63.8 %collective-permute-start.32 = (bf16[1040,1024]{1,0:T(8,128)(2,1)}, bf16[1040,1024]{1,0:T(8,128)(2,1)}, u32[]{:S(2)}, u32[]{:S(2)}) collective-permute-start(bf16[1040,1024]{1,0:T(8,128)(2,1)} %collective-permute-done.31.refs_2_), channel_id=1, source_target_pairs={{0,1},{1,0},{2,3},{3,2},{4,5},{5,4},{6,7},{7,6},{8,9},{9,8},{10,11... | collective-permute-start | bytes 6389768 | tf_op jit(solution)/shard_map/ppermute | solution.py:433
  232.7 54.9 %collective-permute-start.24 = (bf16[3,512,512]{2,1,0:T(8,128)(2,1)}, bf16[3,512,512]{2,1,0:T(8,128)(2,1)}, u32[]{:S(2)}, u32[]{:S(2)}) collective-permute-start(bf16[3,512,512]{2,1,0:T(8,128)(2,1)} %collective-permute-done.23.refs_2_), channel_id=1, source_target_pairs={{0,8},{8,16},{16,24},{24,28},{28,20},{20,12},{12,4},{4,0},{1,9},{9... | collective-permute-start | bytes 4718600 | tf_op jit(solution)/shard_map/ppermute | solution.py:408
  233.6 55.4 %collective-permute-start.26 = (bf16[3,512,512]{2,1,0:T(8,128)(2,1)}, bf16[3,512,512]{2,1,0:T(8,128)(2,1)}, u32[]{:S(2)}, u32[]{:S(2)}) collective-permute-start(bf16[3,512,512]{2,1,0:T(8,128)(2,1)} %collective-permute-done.25.refs_6_), channel_id=1, source_target_pairs={{8,0},{16,8},{24,16},{28,24},{20,28},{12,20},{4,12},{0,4},{9,1},{1... | collective-permute-start | bytes 4718600 | tf_op jit(solution)/shard_map/ppermute | solution.py:409
  252.1 34.9 %collective-permute-start.28 = (bf16[3,512,256]{2,1,0:T(8,128)(2,1)}, bf16[3,512,256]{2,1,0:T(8,128)(2,1)}, u32[]{:S(2)}, u32[]{:S(2)}) collective-permute-start(bf16[3,512,256]{2,1,0:T(8,128)(2,1)} %get-tuple-element.76.refs_0_), channel_id=1, source_target_pairs={{8,0},{16,8},{24,16},{28,24},{20,28},{12,20},{4,12},{0,4},{9,1},{1... | collective-permute-start | bytes 2359304 | tf_op jit(solution)/shard_map/ppermute | solution.py:409
  290.3 34.3 %collective-permute-start.33 = (bf16[3,256,512]{2,1,0:T(8,128)(2,1)S(1)}, bf16[3,256,512]{2,1,0:T(8,128)(2,1)S(1)}, u32[]{:S(2)}, u32[]{:S(2)}) collective-permute-start(bf16[3,256,512]{2,1,0:T(8,128)(2,1)S(1)} %slice.67), channel_id=1, source_target_pairs={{0,8},{8,16},{16,24},{24,28},{28,20},{20,12},{12,4},{4,0},{1,9},{9... | collective-permute-start | bytes 2359304 | tf_op jit(solution)/shard_map/ppermute | solution.py:408
  292.2 33.0 %collective-permute-start.34 = (bf16[3,256,512]{2,1,0:T(8,128)(2,1)S(1)}, bf16[3,256,512]{2,1,0:T(8,128)(2,1)S(1)}, u32[]{:S(2)}, u32[]{:S(2)}) collective-permute-start(bf16[3,256,512]{2,1,0:T(8,128)(2,1)S(1)} %slice.68), channel_id=1, source_target_pairs={{8,0},{16,8},{24,16},{28,24},{20,28},{12,20},{4,12},{0,4},{9,1},{1... | collective-permute-start | bytes 2359304 | tf_op jit(solution)/shard_map/ppermute | solution.py:409
  308.4 38.8 %collective-permute-start.37 = (bf16[3,512,256]{2,1,0:T(8,128)(2,1)S(1)}, bf16[3,512,256]{2,1,0:T(8,128)(2,1)S(1)}, u32[]{:S(2)}, u32[]{:S(2)}) collective-permute-start(bf16[3,512,256]{2,1,0:T(8,128)(2,1)S(1)} %collective-permute-done.35.refs_2_), channel_id=1, source_target_pairs={{0,8},{8,16},{16,24},{24,28},{28,20},{20,12},{12,4},{4,0},{1,9},{9... | collective-permute-start | bytes 2359304 | tf_op jit(solution)/shard_map/ppermute | solution.py:408
  309.3 37.8 %collective-permute-start.38 = (bf16[3,512,256]{2,1,0:T(8,128)(2,1)S(1)}, bf16[3,512,256]{2,1,0:T(8,128)(2,1)S(1)}, u32[]{:S(2)}, u32[]{:S(2)}) collective-permute-start(bf16[3,512,256]{2,1,0:T(8,128)(2,1)S(1)} %collective-permute-done.36.refs_6_), channel_id=1, source_target_pairs={{8,0},{16,8},{24,16},{28,24},{20,28},{12,20},{4,12},{0,4},{9,1},{1... | collective-permute-start | bytes 2359304 | tf_op jit(solution)/shard_map/ppermute | solution.py:409
  325.2 31.2 %collective-permute-start.39 = (bf16[3,512,256]{2,1,0:T(8,128)(2,1)S(1)}, bf16[3,512,256]{2,1,0:T(8,128)(2,1)S(1)}, u32[]{:S(2)}, u32[]{:S(2)}) collective-permute-start(bf16[3,512,256]{2,1,0:T(8,128)(2,1)S(1)} %get-tuple-element.86.refs_0_), channel_id=1, source_target_pairs={{0,8},{8,16},{16,24},{24,28},{28,20},{20,12},{12,4},{4,0},{1,9},{9... | collective-permute-start | bytes 2359304 | tf_op jit(solution)/shard_map/ppermute | solution.py:408
  326.2 30.5 %collective-permute-start.40 = (bf16[3,512,256]{2,1,0:T(8,128)(2,1)S(1)}, bf16[3,512,256]{2,1,0:T(8,128)(2,1)S(1)}, u32[]{:S(2)}, u32[]{:S(2)}) collective-permute-start(bf16[3,512,256]{2,1,0:T(8,128)(2,1)S(1)} %get-tuple-element.86.refs_0_), channel_id=1, source_target_pairs={{8,0},{16,8},{24,16},{28,24},{20,28},{12,20},{4,12},{0,4},{9,1},{1... | collective-permute-start | bytes 2359304 | tf_op jit(solution)/shard_map/ppermute | solution.py:409
  356.8 29.2 %collective-permute-start.41 = (bf16[3,256,256]{2,1,0:T(8,128)(2,1)S(1)}, bf16[3,256,256]{2,1,0:T(8,128)(2,1)S(1)}, u32[]{:S(2)}, u32[]{:S(2)}) collective-permute-start(bf16[3,256,256]{2,1,0:T(8,128)(2,1)S(1)} %slice.70), channel_id=1, source_target_pairs={{0,8},{8,16},{16,24},{24,28},{28,20},{20,12},{12,4},{4,0},{1,9},{9... | collective-permute-start | bytes 1179656 | tf_op jit(solution)/shard_map/ppermute | solution.py:408
  358.1 27.8 %collective-permute-start.42 = (bf16[3,256,256]{2,1,0:T(8,128)(2,1)S(1)}, bf16[3,256,256]{2,1,0:T(8,128)(2,1)S(1)}, u32[]{:S(2)}, u32[]{:S(2)}) collective-permute-start(bf16[3,256,256]{2,1,0:T(8,128)(2,1)S(1)} %slice.71), channel_id=1, source_target_pairs={{8,0},{16,8},{24,16},{28,24},{20,28},{12,20},{4,12},{0,4},{9,1},{1... | collective-permute-start | bytes 1179656 | tf_op jit(solution)/shard_map/ppermute | solution.py:409
  360.1 23.8 %collective-permute-start.44 = (bf16[3,512,256]{2,1,0:T(8,128)(2,1)S(1)}, bf16[3,512,256]{2,1,0:T(8,128)(2,1)S(1)}, u32[]{:S(2)}, u32[]{:S(2)}) collective-permute-start(bf16[3,512,256]{2,1,0:T(8,128)(2,1)S(1)} %collective-permute-done.40.refs_5_), channel_id=1, source_target_pairs={{8,0},{16,8},{24,16},{28,24},{20,28},{12,20},{4,12},{0,4},{9,1},{1... | collective-permute-start | bytes 2359304 | tf_op jit(solution)/shard_map/ppermute | solution.py:409
  (83 other events, 1443.7 us)
